TPU v7x, 32 devices: a whole 2x2x4 slice. The times are simulated.
32 devices in a mesh: shot: 4 (over x, core), dom: 8 (over z, y).
Axes of the slice: x: 2, y: 2, z: 4, core: 2. Of those that a mesh axis runs over, the one named last changes fastest.
Arguments:
- parked: bfloat16 [4, 64, 32768], P('shot', 'dom'), may hold values from -6 to 6
- parked_slot: int32 [4, 8, 8], P('shot', 'dom'), may hold values from 0 to 7, as said below
- holder_list: int32 [4, 8, 8], P('shot', 'dom'), may hold values from 0 to 7, as said below
- speed_sq: float32 [64, 128, 128], P('dom'), may hold values from 0.04 to 0.18
- adjoint_next: float32 [4, 64, 128, 128], P('shot', 'dom'), may hold values from -6 to 6
- adjoint_now: float32 [4, 64, 128, 128], P('shot', 'dom'), may hold values from -6 to 6
- wavelet: float32 [4, 3], P('shot'), may hold values from -9 to 9
- src_depth: int32 [4], P('shot'), may hold values from 0 to 63
- src_row: int32 [4], P('shot'), may hold values from 0 to 16383
- rec_depth: int32 [1024], replicated, may hold values from 0 to 63
- rec_row: int32 [1024], replicated, may hold values from 0 to 16383
- residuals: float32 [4, 4, 1024], P('shot'), may hold values from -6 to 6
Outputs:
- gradient: float32 [64, 128, 128], P('dom', 'shot')
- adjoint_late: float32 [4, 64, 128, 128], P('shot', 'dom')
- adjoint_early: float32 [4, 64, 128, 128], P('shot', 'dom')
Inputs may be any that keep to these rules, and one draw needn't show every extreme that they name: Each row of parked_slot names every slot of its holder once. Each row of holder_list names every holder slab once.
All inputs are finite; a program needn't handle non-finite values.
Results may differ from a plain program's by a relative error of at most 0.0005.
Values may be sent and summed in bfloat16 or wider, within the bound.
A program may use at most 64 MiB of HBM per device.

v0:
```python
import jax
import jax.numpy as jnp
from jax import lax
from jax.sharding import PartitionSpec as P

STEPS = 4


stencil_coef = (-205.0 / 72.0, 8.0 / 5.0, -1.0 / 5.0, 8.0 / 315.0, -1.0 / 560.0)
grad_scale = 0.0625


def extended_2(value, sides, width):
    for axis, dim in sides:
        peers, length = (lax.axis_size(axis), value.shape[dim])
        up = [(i, (i + 1) % peers) for i in range(peers - 1)]
        down = [(j, i) for i, j in up]
        last = lax.slice_in_dim(value, length - width, length, axis=dim)
        initial = lax.slice_in_dim(value, 0, width, axis=dim)
        before = lax.ppermute(last, axis, up)
        after = lax.ppermute(initial, axis, down)
        value = jnp.concatenate([before, value, after], axis=dim)
    return value


def lateral(field):
    width_x, width_y = (field.shape[1], field.shape[2])
    padded = jnp.pad(field, ((0, 0), (4, 4), (4, 4)))
    summed = 3.0 * stencil_coef[0] * field
    for offset in range(1, 5):
        neighbours = (
            padded[:, 4 + offset : 4 + offset + width_x, 4 : 4 + width_y]
            + padded[:, 4 - offset : 4 - offset + width_x, 4 : 4 + width_y]
        )
        neighbours = (
            neighbours
            + padded[:, 4 : 4 + width_x, 4 + offset : 4 + offset + width_y]
            + padded[:, 4 : 4 + width_x, 4 - offset : 4 - offset + width_y]
        )
        summed = summed + stencil_coef[offset] * neighbours
    return summed


def vertical(extended, slab_depth):
    summed = stencil_coef[1] * (extended[5 : 5 + slab_depth] + extended[3 : 3 + slab_depth])
    for offset in range(2, 5):
        summed = summed + stencil_coef[offset] * (
            extended[4 + offset : 4 + offset + slab_depth]
            + extended[4 - offset : 4 - offset + slab_depth]
        )
    return summed


def laplace(field, extended):
    return lateral(field) + vertical(extended, field.shape[0])


def inject(field, depth_at, row_at, amount, top_plane):
    slab_depth, width_x, width_y = field.shape
    local_depth = depth_at - top_plane
    inside = (local_depth >= 0) & (local_depth < slab_depth)
    flat_index = jnp.clip(local_depth, 0, slab_depth - 1) * (width_x * width_y) + row_at
    updated = field.reshape(-1).at[flat_index].add(jnp.where(inside, amount, 0.0))
    return updated.reshape(slab_depth, width_x, width_y)


def per_device(
    parked,
    parked_slot,
    holder_list,
    speed_sq,
    adjoint_next,
    adjoint_now,
    wavelet,
    src_depth,
    src_row,
    rec_depth,
    rec_row,
    residuals,
):
    slab_depth, width_x, width_y = speed_sq.shape
    top_plane = lax.axis_index("dom") * slab_depth
    outgoing = jnp.take(parked[0], parked_slot[0, 0], axis=0)
    incoming = lax.all_to_all(outgoing, "dom", split_axis=0, concat_axis=0, tiled=True)
    pieces = jnp.take(incoming, holder_list[0, 0], axis=0)
    stored = pieces.reshape(2, slab_depth, width_x, width_y).astype(jnp.float32)
    previous = stored[0]
    current = stored[1]
    adj_later = adjoint_next[0]
    present = adjoint_now[0]
    forward_laps = []
    adjoint_fields = []
    for step_num in range(STEPS):
        extended = extended_2(current, (("dom", 0),), 4)
        lap_forward = laplace(current, extended)
        forward_laps.append(lap_forward)
        if step_num + 1 < STEPS:
            forward_advanced = 2.0 * current - previous + speed_sq * lap_forward
            previous, current = (
                current,
                inject(
                    forward_advanced,
                    src_depth,
                    src_row,
                    wavelet[0, step_num : step_num + 1],
                    top_plane,
                ),
            )
    for step_num in range(STEPS):
        scaled = speed_sq * present
        extended = extended_2(scaled, (("dom", 0),), 4)
        lap_adjoint = laplace(scaled, extended)
        adjoint_fields.append(present)
        advanced = 2.0 * present - adj_later + lap_adjoint
        adj_later, present = (
            present,
            inject(advanced, rec_depth, rec_row, residuals[0, step_num], top_plane),
        )
    summed = adjoint_fields[0] * forward_laps[STEPS - 1]
    for step_num in range(1, STEPS):
        summed = summed + adjoint_fields[step_num] * forward_laps[STEPS - 1 - step_num]
    gradient = lax.psum_scatter(grad_scale * summed, "shot", scatter_dimension=1, tiled=True)
    return (gradient, adj_later[None], present[None])


def solution(mesh):
    in_specs = (
        P("shot", "dom", None),
        P("shot", "dom", None),
        P("shot", "dom", None),
        P("dom", None, None),
        P("shot", "dom", None, None),
        P("shot", "dom", None, None),
        P("shot", None),
        P("shot"),
        P("shot"),
        P(),
        P(),
        P("shot", None, None),
    )
    out_specs = (P("dom", "shot", None), P("shot", "dom", None, None), P("shot", "dom", None, None))
    return jax.shard_map(
        per_device, mesh=mesh, in_specs=in_specs, out_specs=out_specs, check_vma=False
    )
```

profile of v0, /device:TPU:0, one launch (start us, length us, event | category | flops | bytes accessed | tf_op | source)
XLA Modules:
  0.0 195.0 jit_solution(15976370584505944914)
XLA Ops:
  12.4 7.3 %all-to-all-start = ((bf16[8,2,16384]{2,1,0:T(2,128)(2,1)}), bf16[8,2,16384]{2,1,0:T(2,128)(2,1)S(1)}, u32[]{:S(2)}, u32[]{:S(2)}) async-start(bf16[8,2,16384]{2,1,0:T(2,128)(2,1)} %reshape.240), calls=%async_computation | async-start | bytes 1048576 | tf_op jit(solution)/shard_map/all_to_all | solution.py:84
  22.2 11.9 %all-to-all-done = bf16[8,2,16384]{2,1,0:T(2,128)(2,1)S(1)} async-done(((bf16[8,2,16384]{2,1,0:T(2,128)(2,1)}), bf16[8,2,16384]{2,1,0:T(2,128)(2,1)S(1)}, u32[]{:S(2)}, u32[]{:S(2)}) %all-to-all-start) | async-done | bytes 524320 | tf_op jit(solution)/shard_map/all_to_all | solution.py:84
  38.6 5.3 %collective-permute-start.1 = (f32[4,128,128]{2,1,0:T(8,128)}, f32[4,128,128]{2,1,0:T(8,128)}, u32[]{:S(2)}, u32[]{:S(2)}) collective-permute-start(f32[4,128,128]{2,1,0:T(8,128)} %get-tuple-element.49), channel_id=1, source_target_pairs={{0,1},{1,2},{2,3},{3,4},{4,5},{5,6},{6,7},{8,9},{9,10},{10,11},{11... | collective-permute-start | bytes 786440 | tf_op jit(solution)/shard_map/ppermute | solution.py:20
  45.5 6.7 %collective-permute-done.1 = f32[4,128,128]{2,1,0:T(8,128)} collective-permute-done((f32[4,128,128]{2,1,0:T(8,128)}, f32[4,128,128]{2,1,0:T(8,128)}, u32[]{:S(2)}, u32[]{:S(2)}) %collective-permute-start.1) | collective-permute-done | bytes 262176 | tf_op jit(solution)/shard_map/ppermute | solution.py:20
  58.0 5.0 %collective-permute-start.9 = (f32[4,128,128]{2,1,0:T(8,128)S(1)}, f32[4,128,128]{2,1,0:T(8,128)S(1)}, u32[]{:S(2)}, u32[]{:S(2)}) collective-permute-start(f32[4,128,128]{2,1,0:T(8,128)S(1)} %get-tuple-element.63), channel_id=1, source_target_pairs={{0,1},{1,2},{2,3},{3,4},{4,5},{5,6},{6,7},{8,9},{9,10},{10,11},{11... | collective-permute-start | bytes 786440 | tf_op jit(solution)/shard_map/ppermute | solution.py:20
  63.0 2.0 %fusion.303 = f32[131072]{0:T(1024)S(1)} fusion(f32[131072]{0:T(1024)S(1)} %bitcast.88, s32[]{:T(128)} %bitcast.9, f32[1,1]{1,0:T(1,128)} %get-tuple-element.81, s32[1]{0:T(128)} %compare_select_fusion.3, s32[1]{0:T(128)S(6)} %copy.30, s32[1]{0:T(128)} %bitcast.8), kind=kLoop, calls=%fused_computation.573 | loop fusion | flops 10 | bytes 1044 | tf_op jit(solution)/shard_map/scatter-add | solution.py:63
  65.8 4.8 %collective-permute-start.3 = (f32[4,128,128]{2,1,0:T(8,128)}, f32[4,128,128]{2,1,0:T(8,128)S(1)}, u32[]{:S(2)}, u32[]{:S(2)}) collective-permute-start(f32[4,128,128]{2,1,0:T(8,128)} %bitcast.13), channel_id=1, source_target_pairs={{0,1},{1,2},{2,3},{3,4},{4,5},{5,6},{6,7},{8,9},{9,10},{10,11},{11... | collective-permute-start | bytes 786440 | tf_op jit(solution)/shard_map/ppermute | solution.py:20
  74.6 6.3 %scatter_fusion = f32[131072]{0:T(1024)S(1)} fusion(f32[131072]{0:T(1024)S(1)} %bitcast.71, s32[1024]{0:T(1024)S(1)} %compare_select_fusion, f32[1024]{0:T(1024)S(1)} %get-tuple-element.79), kind=kCustom, calls=%fused_computation.2 | custom fusion | flops 1024 | bytes 16384 | tf_op jit(solution)/shard_map/scatter-add | solution.py:63
  80.8 3.8 %collective-permute-done.3 = f32[4,128,128]{2,1,0:T(8,128)S(1)} collective-permute-done((f32[4,128,128]{2,1,0:T(8,128)}, f32[4,128,128]{2,1,0:T(8,128)S(1)}, u32[]{:S(2)}, u32[]{:S(2)}) %collective-permute-start.3) | collective-permute-done | bytes 262176 | tf_op jit(solution)/shard_map/ppermute | solution.py:20
  84.7 2.9 %multiply_add_fusion.1 = (f32[8,128,128]{2,1,0:T(8,128)S(1)}, f32[8,128,128]{2,1,0:T(8,128)}, f32[8,128,128]{2,1,0:T(8,128)S(1)}) fusion(f32[8,128,128]{2,1,0:T(8,128)S(1)} %copy-done.4, f32[8,128,128]{2,1,0:T(8,128)S(1)} %squeeze.46, f32[8,128,128]{2,1,0:T(8,128)S(1)} %bitcast.89, f32[4,128,128]{2,1,0:T(8,128)S(1)} %collective-permute-done.3, ...), kind=kLoop, calls=%fused_computation.547 | loop fusion | flops 6029312 | bytes 4194304 | tf_op jit(solution)/shard_map/add | solution.py:98
  89.0 6.9 %collective-permute-start.11 = (f32[4,128,128]{2,1,0:T(8,128)S(1)}, f32[4,128,128]{2,1,0:T(8,128)S(1)}, u32[]{:S(2)}, u32[]{:S(2)}) collective-permute-start(f32[4,128,128]{2,1,0:T(8,128)S(1)} %get-tuple-element.60), channel_id=1, source_target_pairs={{0,1},{1,2},{2,3},{3,4},{4,5},{5,6},{6,7},{8,9},{9,10},{10,11},{11... | collective-permute-start | bytes 786440 | tf_op jit(solution)/shard_map/ppermute | solution.py:20
  98.7 4.8 %collective-permute-start.5 = (f32[4,128,128]{2,1,0:T(8,128)}, f32[4,128,128]{2,1,0:T(8,128)S(1)}, u32[]{:S(2)}, u32[]{:S(2)}) collective-permute-start(f32[4,128,128]{2,1,0:T(8,128)} %bitcast.18), channel_id=1, source_target_pairs={{0,1},{1,2},{2,3},{3,4},{4,5},{5,6},{6,7},{8,9},{9,10},{10,11},{11... | collective-permute-start | bytes 786440 | tf_op jit(solution)/shard_map/ppermute | solution.py:20
  106.0 6.5 %scatter_fusion.1 = f32[131072]{0:T(1024)S(1)} fusion(f32[131072]{0:T(1024)S(1)} %bitcast.76, s32[1024]{0:T(1024)S(1)} %compare_select_fusion, f32[1024]{0:T(1024)S(1)} %get-tuple-element.78), kind=kCustom, calls=%fused_computation.3 | custom fusion | flops 1024 | bytes 16384 | tf_op jit(solution)/shard_map/scatter-add | solution.py:63
  112.4 3.1 %collective-permute-done.5 = f32[4,128,128]{2,1,0:T(8,128)S(1)} collective-permute-done((f32[4,128,128]{2,1,0:T(8,128)}, f32[4,128,128]{2,1,0:T(8,128)S(1)}, u32[]{:S(2)}, u32[]{:S(2)}) %collective-permute-start.5) | collective-permute-done | bytes 262176 | tf_op jit(solution)/shard_map/ppermute | solution.py:20
  115.6 8.9 %multiply_add_fusion = (f32[8,128,128]{2,1,0:T(8,128)S(1)}, f32[8,128,128]{2,1,0:T(8,128)}, f32[8,128,128]{2,1,0:T(8,128)S(1)}) fusion(f32[8,128,128]{2,1,0:T(8,128)S(1)} %copy-done.4, f32[8,128,128]{2,1,0:T(8,128)S(1)} %bitcast.90, f32[8,128,128]{2,1,0:T(8,128)} %bitcast.94, f32[4,128,128]{2,1,0:T(8,128)S(1)} %collective-permute-done.5, ...), kind=kLoop, calls=%fused_computation.546 | loop fusion | flops 6029312 | bytes 4194304 | tf_op jit(solution)/shard_map/add | solution.py:98
  125.8 4.9 %collective-permute-start.13 = (f32[4,128,128]{2,1,0:T(8,128)S(1)}, f32[4,128,128]{2,1,0:T(8,128)S(1)}, u32[]{:S(2)}, u32[]{:S(2)}) collective-permute-start(f32[4,128,128]{2,1,0:T(8,128)S(1)} %get-tuple-element.57), channel_id=1, source_target_pairs={{0,1},{1,2},{2,3},{3,4},{4,5},{5,6},{6,7},{8,9},{9,10},{10,11},{11... | collective-permute-start | bytes 786440 | tf_op jit(solution)/shard_map/ppermute | solution.py:20
  133.5 4.8 %collective-permute-start.7 = (f32[4,128,128]{2,1,0:T(8,128)}, f32[4,128,128]{2,1,0:T(8,128)S(1)}, u32[]{:S(2)}, u32[]{:S(2)}) collective-permute-start(f32[4,128,128]{2,1,0:T(8,128)} %bitcast.23), channel_id=1, source_target_pairs={{0,1},{1,2},{2,3},{3,4},{4,5},{5,6},{6,7},{8,9},{9,10},{10,11},{11... | collective-permute-start | bytes 786440 | tf_op jit(solution)/shard_map/ppermute | solution.py:20
  142.2 6.3 %scatter_fusion.2 = f32[131072]{0:T(1024)S(1)} fusion(f32[131072]{0:T(1024)S(1)} %bitcast.81, s32[1024]{0:T(1024)S(1)} %compare_select_fusion, f32[1024]{0:T(1024)S(1)} %get-tuple-element.77), kind=kCustom, calls=%fused_computation.4 | custom fusion | flops 1024 | bytes 16384 | tf_op jit(solution)/shard_map/scatter-add | solution.py:63
  148.5 3.8 %collective-permute-done.7 = f32[4,128,128]{2,1,0:T(8,128)S(1)} collective-permute-done((f32[4,128,128]{2,1,0:T(8,128)}, f32[4,128,128]{2,1,0:T(8,128)S(1)}, u32[]{:S(2)}, u32[]{:S(2)}) %collective-permute-start.7) | collective-permute-done | bytes 262176 | tf_op jit(solution)/shard_map/ppermute | solution.py:20
  152.3 9.9 %fusion.311 = (f32[8,128,128]{2,1,0:T(8,128)}, f32[8,128,128]{2,1,0:T(8,128)}) fusion(f32[8,128,128]{2,1,0:T(8,128)S(1)} %copy-done.4, f32[8,128,128]{2,1,0:T(8,128)S(1)} %bitcast.82, f32[8,128,128]{2,1,0:T(8,128)} %get-tuple-element.47, f32[8,128,128]{2,1,0:T(8,128)S(1)} %bitcast.79, f32[8,128,128]{2,1,0:T(8,128)} %get-tuple-element.45, ...), kind=kLoop, calls=%fused_computation.581 | loop fusion | flops 6553600 | bytes 6291456 | tf_op jit(solution)/shard_map/mul | solution.py:110
  164.7 6.9 %collective-permute-start.15 = (f32[4,128,128]{2,1,0:T(8,128)S(1)}, f32[4,128,128]{2,1,0:T(8,128)S(1)}, u32[]{:S(2)}, u32[]{:S(2)}) collective-permute-start(f32[4,128,128]{2,1,0:T(8,128)S(1)} %get-tuple-element.53), channel_id=1, source_target_pairs={{0,1},{1,2},{2,3},{3,4},{4,5},{5,6},{6,7},{8,9},{9,10},{10,11},{11... | collective-permute-start | bytes 786440 | tf_op jit(solution)/shard_map/ppermute | solution.py:20
  171.6 2.6 %collective-permute-done.14 = f32[4,128,128]{2,1,0:T(8,128)S(1)} collective-permute-done((f32[4,128,128]{2,1,0:T(8,128)S(1)}, f32[4,128,128]{2,1,0:T(8,128)S(1)}, u32[]{:S(2)}, u32[]{:S(2)}) %collective-permute-start.14) | collective-permute-done | bytes 262176 | tf_op jit(solution)/shard_map/ppermute | solution.py:21
  174.1 5.8 %collective-permute-done.15 = f32[4,128,128]{2,1,0:T(8,128)S(1)} collective-permute-done((f32[4,128,128]{2,1,0:T(8,128)S(1)}, f32[4,128,128]{2,1,0:T(8,128)S(1)}, u32[]{:S(2)}, u32[]{:S(2)}) %collective-permute-start.15) | collective-permute-done | bytes 262176 | tf_op jit(solution)/shard_map/ppermute | solution.py:20
  181.1 6.3 %scatter_fusion.3 = f32[131072]{0:T(1024)S(1)} fusion(f32[131072]{0:T(1024)S(1)} %bitcast.85, s32[1024]{0:T(1024)S(1)} %compare_select_fusion, f32[1024]{0:T(1024)S(1)} %get-tuple-element.40), kind=kCustom, calls=%fused_computation.5 | custom fusion | flops 1024 | bytes 16384 | tf_op jit(solution)/shard_map/scatter-add | solution.py:63
  (93 shorter events, 41.3 us)
Async XLA Ops:
  11.1 11.0 %copy-start.10 = (s32[1024]{0:T(1024)S(1)}, s32[1024]{0:T(1024)}, u32[]{:S(2)}) copy-start(s32[1024]{0:T(1024)} %param.29) | copy-start | bytes 12292
  11.2 11.0 %copy-start.13 = (s32[1024]{0:T(1024)S(1)}, s32[1024]{0:T(1024)}, u32[]{:S(2)}) copy-start(s32[1024]{0:T(1024)} %param.30) | copy-start | bytes 12292
  11.2 11.0 %copy-start.11 = (f32[1,4,1024]{2,1,0:T(4,128)S(1)}, f32[1,4,1024]{2,1,0:T(4,128)}, u32[]{:S(2)}) copy-start(f32[1,4,1024]{2,1,0:T(4,128)} %param.31) | copy-start | bytes 49156
  12.4 21.8 %all-to-all-start = ((bf16[8,2,16384]{2,1,0:T(2,128)(2,1)}), bf16[8,2,16384]{2,1,0:T(2,128)(2,1)S(1)}, u32[]{:S(2)}, u32[]{:S(2)}) async-start(bf16[8,2,16384]{2,1,0:T(2,128)(2,1)} %reshape.240), calls=%async_computation | async-start | bytes 1048576 | tf_op jit(solution)/shard_map/all_to_all | solution.py:84
  19.6 167.7 %reduce-scatter.2.cloned.1.call-start = ((), (), s32[]{:S(2)}) async-start(), calls=%async_computation.2 | async-start | bytes 655360 | tf_op jit(solution)/shard_map/reduce_scatter | solution.py:122
  37.3 16.1 %collective-permute-start = (f32[4,128,128]{2,1,0:T(8,128)}, f32[4,128,128]{2,1,0:T(8,128)S(1)}, u32[]{:S(2)}, u32[]{:S(2)}) collective-permute-start(f32[4,128,128]{2,1,0:T(8,128)} %get-tuple-element.48), channel_id=1, source_target_pairs={{1,0},{2,1},{3,2},{4,3},{5,4},{6,5},{7,6},{9,8},{10,9},{11,10},{12... | collective-permute-start | bytes 786440 | tf_op jit(solution)/shard_map/ppermute | solution.py:21
  38.6 13.7 %collective-permute-start.1 = (f32[4,128,128]{2,1,0:T(8,128)}, f32[4,128,128]{2,1,0:T(8,128)}, u32[]{:S(2)}, u32[]{:S(2)}) collective-permute-start(f32[4,128,128]{2,1,0:T(8,128)} %get-tuple-element.49), channel_id=1, source_target_pairs={{0,1},{1,2},{2,3},{3,4},{4,5},{5,6},{6,7},{8,9},{9,10},{10,11},{11... | collective-permute-start | bytes 786440 | tf_op jit(solution)/shard_map/ppermute | solution.py:20
  56.5 16.9 %copy-start.9 = (f32[1,8,128,128]{3,2,1,0:T(8,128)S(1)}, f32[1,8,128,128]{3,2,1,0:T(8,128)}, u32[]{:S(2)}) copy-start(f32[1,8,128,128]{3,2,1,0:T(8,128)} %param.24) | copy-start | bytes 1572868
  56.6 15.4 %collective-permute-start.8 = (f32[4,128,128]{2,1,0:T(8,128)S(1)}, f32[4,128,128]{2,1,0:T(8,128)S(1)}, u32[]{:S(2)}, u32[]{:S(2)}) collective-permute-start(f32[4,128,128]{2,1,0:T(8,128)S(1)} %get-tuple-element.62), channel_id=1, source_target_pairs={{1,0},{2,1},{3,2},{4,3},{5,4},{6,5},{7,6},{9,8},{10,9},{11,10},{12... | collective-permute-start | bytes 786440 | tf_op jit(solution)/shard_map/ppermute | solution.py:21
  58.0 15.4 %collective-permute-start.9 = (f32[4,128,128]{2,1,0:T(8,128)S(1)}, f32[4,128,128]{2,1,0:T(8,128)S(1)}, u32[]{:S(2)}, u32[]{:S(2)}) collective-permute-start(f32[4,128,128]{2,1,0:T(8,128)S(1)} %get-tuple-element.63), channel_id=1, source_target_pairs={{0,1},{1,2},{2,3},{3,4},{4,5},{5,6},{6,7},{8,9},{9,10},{10,11},{11... | collective-permute-start | bytes 786440 | tf_op jit(solution)/shard_map/ppermute | solution.py:20
  65.8 18.9 %collective-permute-start.3 = (f32[4,128,128]{2,1,0:T(8,128)}, f32[4,128,128]{2,1,0:T(8,128)S(1)}, u32[]{:S(2)}, u32[]{:S(2)}) collective-permute-start(f32[4,128,128]{2,1,0:T(8,128)} %bitcast.13), channel_id=1, source_target_pairs={{0,1},{1,2},{2,3},{3,4},{4,5},{5,6},{6,7},{8,9},{9,10},{10,11},{11... | collective-permute-start | bytes 786440 | tf_op jit(solution)/shard_map/ppermute | solution.py:20
  70.6 14.1 %collective-permute-start.2 = (f32[4,128,128]{2,1,0:T(8,128)}, f32[4,128,128]{2,1,0:T(8,128)}, u32[]{:S(2)}, u32[]{:S(2)}) collective-permute-start(f32[4,128,128]{2,1,0:T(8,128)} %bitcast.12), channel_id=1, source_target_pairs={{1,0},{2,1},{3,2},{4,3},{5,4},{6,5},{7,6},{9,8},{10,9},{11,10},{12... | collective-permute-start | bytes 786440 | tf_op jit(solution)/shard_map/ppermute | solution.py:21
  87.7 17.1 %collective-permute-start.10 = (f32[4,128,128]{2,1,0:T(8,128)S(1)}, f32[4,128,128]{2,1,0:T(8,128)S(1)}, u32[]{:S(2)}, u32[]{:S(2)}) collective-permute-start(f32[4,128,128]{2,1,0:T(8,128)S(1)} %get-tuple-element.59), channel_id=1, source_target_pairs={{1,0},{2,1},{3,2},{4,3},{5,4},{6,5},{7,6},{9,8},{10,9},{11,10},{12... | collective-permute-start | bytes 786440 | tf_op jit(solution)/shard_map/ppermute | solution.py:21
  89.0 15.8 %collective-permute-start.11 = (f32[4,128,128]{2,1,0:T(8,128)S(1)}, f32[4,128,128]{2,1,0:T(8,128)S(1)}, u32[]{:S(2)}, u32[]{:S(2)}) collective-permute-start(f32[4,128,128]{2,1,0:T(8,128)S(1)} %get-tuple-element.60), channel_id=1, source_target_pairs={{0,1},{1,2},{2,3},{3,4},{4,5},{5,6},{6,7},{8,9},{9,10},{10,11},{11... | collective-permute-start | bytes 786440 | tf_op jit(solution)/shard_map/ppermute | solution.py:20
  98.7 16.9 %collective-permute-start.5 = (f32[4,128,128]{2,1,0:T(8,128)}, f32[4,128,128]{2,1,0:T(8,128)S(1)}, u32[]{:S(2)}, u32[]{:S(2)}) collective-permute-start(f32[4,128,128]{2,1,0:T(8,128)} %bitcast.18), channel_id=1, source_target_pairs={{0,1},{1,2},{2,3},{3,4},{4,5},{5,6},{6,7},{8,9},{9,10},{10,11},{11... | collective-permute-start | bytes 786440 | tf_op jit(solution)/shard_map/ppermute | solution.py:20
  103.5 12.1 %collective-permute-start.4 = (f32[4,128,128]{2,1,0:T(8,128)}, f32[4,128,128]{2,1,0:T(8,128)}, u32[]{:S(2)}, u32[]{:S(2)}) collective-permute-start(f32[4,128,128]{2,1,0:T(8,128)} %bitcast.17), channel_id=1, source_target_pairs={{1,0},{2,1},{3,2},{4,3},{5,4},{6,5},{7,6},{9,8},{10,9},{11,10},{12... | collective-permute-start | bytes 786440 | tf_op jit(solution)/shard_map/ppermute | solution.py:21
  124.5 15.1 %collective-permute-start.12 = (f32[4,128,128]{2,1,0:T(8,128)S(1)}, f32[4,128,128]{2,1,0:T(8,128)S(1)}, u32[]{:S(2)}, u32[]{:S(2)}) collective-permute-start(f32[4,128,128]{2,1,0:T(8,128)S(1)} %get-tuple-element.56), channel_id=1, source_target_pairs={{1,0},{2,1},{3,2},{4,3},{5,4},{6,5},{7,6},{9,8},{10,9},{11,10},{12... | collective-permute-start | bytes 786440 | tf_op jit(solution)/shard_map/ppermute | solution.py:21
  125.8 15.3 %collective-permute-start.13 = (f32[4,128,128]{2,1,0:T(8,128)S(1)}, f32[4,128,128]{2,1,0:T(8,128)S(1)}, u32[]{:S(2)}, u32[]{:S(2)}) collective-permute-start(f32[4,128,128]{2,1,0:T(8,128)S(1)} %get-tuple-element.57), channel_id=1, source_target_pairs={{0,1},{1,2},{2,3},{3,4},{4,5},{5,6},{6,7},{8,9},{9,10},{10,11},{11... | collective-permute-start | bytes 786440 | tf_op jit(solution)/shard_map/ppermute | solution.py:20
  133.5 18.8 %collective-permute-start.7 = (f32[4,128,128]{2,1,0:T(8,128)}, f32[4,128,128]{2,1,0:T(8,128)S(1)}, u32[]{:S(2)}, u32[]{:S(2)}) collective-permute-start(f32[4,128,128]{2,1,0:T(8,128)} %bitcast.23), channel_id=1, source_target_pairs={{0,1},{1,2},{2,3},{3,4},{4,5},{5,6},{6,7},{8,9},{9,10},{10,11},{11... | collective-permute-start | bytes 786440 | tf_op jit(solution)/shard_map/ppermute | solution.py:20
  138.3 14.0 %collective-permute-start.6 = (f32[4,128,128]{2,1,0:T(8,128)}, f32[4,128,128]{2,1,0:T(8,128)}, u32[]{:S(2)}, u32[]{:S(2)}) collective-permute-start(f32[4,128,128]{2,1,0:T(8,128)} %bitcast.22), channel_id=1, source_target_pairs={{1,0},{2,1},{3,2},{4,3},{5,4},{6,5},{7,6},{9,8},{10,9},{11,10},{12... | collective-permute-start | bytes 786440 | tf_op jit(solution)/shard_map/ppermute | solution.py:21
  148.5 31.4 %copy-start.1 = (f32[131072]{0:T(1024)}, f32[131072]{0:T(1024)S(1)}, u32[]{:S(2)}) copy-start(f32[131072]{0:T(1024)S(1)} %scatter_fusion.2) | copy-start | bytes 1572868
  162.2 17.7 %copy-start.7 = (f32[8,128,128]{2,1,0:T(8,128)S(1)}, f32[8,128,128]{2,1,0:T(8,128)}, u32[]{:S(2)}) copy-start(f32[8,128,128]{2,1,0:T(8,128)} %get-tuple-element.54) | copy-start | bytes 1572868
  163.4 10.8 %collective-permute-start.14 = (f32[4,128,128]{2,1,0:T(8,128)S(1)}, f32[4,128,128]{2,1,0:T(8,128)S(1)}, u32[]{:S(2)}, u32[]{:S(2)}) collective-permute-start(f32[4,128,128]{2,1,0:T(8,128)S(1)} %get-tuple-element.52), channel_id=1, source_target_pairs={{1,0},{2,1},{3,2},{4,3},{5,4},{6,5},{7,6},{9,8},{10,9},{11,10},{12... | collective-permute-start | bytes 786440 | tf_op jit(solution)/shard_map/ppermute | solution.py:21
  164.7 15.2 %collective-permute-start.15 = (f32[4,128,128]{2,1,0:T(8,128)S(1)}, f32[4,128,128]{2,1,0:T(8,128)S(1)}, u32[]{:S(2)}, u32[]{:S(2)}) collective-permute-start(f32[4,128,128]{2,1,0:T(8,128)S(1)} %get-tuple-element.53), channel_id=1, source_target_pairs={{0,1},{1,2},{2,3},{3,4},{4,5},{5,6},{6,7},{8,9},{9,10},{10,11},{11... | collective-permute-start | bytes 786440 | tf_op jit(solution)/shard_map/ppermute | solution.py:20
  (9 other events, 40.8 us)
Sparse Core Ops, SparseCore 0:
  162.4 22.6 reduce-scatter.1
where the time goes:
time: 196 us; the launch traced here: 195 us
  other arithmetic  62 us (32%)
  starting transfers between devices  61.2 us (31%)
  waiting for transfers between devices  40.7 us (21%)
  between operations  16.3 us (8%)
  local copies, waits for them, and re-layouts  14.8 us (8%)
    ppermute x8, starting transfers between devices, extended_2(): before = lax.ppermute(last, axis, up)  43.4 us
    scatter-add x7, other arithmetic, inject(): field.reshape(-1).at[flat_index].add(jnp.where(inside, amount, 0.0))  31 us
    ppermute x8, waiting for transfers between devices, extended_2(): before = lax.ppermute(last, axis, up)  26.2 us
    add x3, other arithmetic, per_device(): forward_advanced = 2.0 * current - previous + speed_sq * lap_forward  13.8 us
    all_to_all x1, waiting for transfers between devices, per_device(): lax.all_to_all(outgoing, 'dom', split_axis=0, concat_axis=0, tiled=True)  11.9 us
    ppermute x8, starting transfers between devices, extended_2(): after = lax.ppermute(initial, axis, down)  10.5 us
    mul x1, other arithmetic, per_device(): scaled = speed_sq * present  9.87 us
    all_to_all x1, starting transfers between devices, per_device(): lax.all_to_all(outgoing, 'dom', split_axis=0, concat_axis=0, tiled=True)  7.28 us
  transfers between devices with their start and end apart: 18, of which 9 were waited for; matrix products, arithmetic and copies ran while one was open for 22% of the time, Pallas kernels for 0%

commit v1 on v0

v1 whole, which is shorter than its diff:
```python
import functools

import jax
import jax.numpy as jnp
from jax import lax
from jax.experimental import pallas as pl
from jax.experimental.pallas import tpu as pltpu
from jax.sharding import PartitionSpec as P

STEPS = 4
HALO = 4
PAD = 8

stencil_coef = (-205.0 / 72.0, 8.0 / 5.0, -1.0 / 5.0, 8.0 / 315.0, -1.0 / 560.0)
grad_scale = 0.0625

MESH = pl.DeviceIdType.MESH
F32 = jnp.float32
BF16 = jnp.bfloat16


def split3(value):
    high = value.astype(BF16)
    rest = value - high.astype(F32)
    mid = rest.astype(BF16)
    low = (rest - mid.astype(F32)).astype(BF16)
    return high, mid, low


def window_kernel(
    n_shot,
    n_dom,
    parked,
    slot,
    ints,
    speed_in,
    next_in,
    now_in,
    floats,
    rec_depth,
    rec_row,
    grad_out,
    late_out,
    early_out,
    send_buf,
    recv_buf,
    ints_w,
    ints_s,
    floats_w,
    speed,
    lam_next,
    lam,
    u_first,
    v_buf,
    e_buf,
    lap,
    lap_adj,
    band,
    parts,
    inject,
    src_mask,
    grad_send,
    grad_recv,
    lam_out,
    a2a_send,
    a2a_recv,
    swap_send,
    swap_recv,
    halo_send,
    halo_recv,
    grad_ssem,
    grad_rsem,
    local_sem,
):
    depth, width, lanes = speed_in.shape
    groups = n_shot // 2
    share = width // n_shot
    n_rec = rec_depth.shape[1]
    shot = lax.axis_index("shot")
    dom = lax.axis_index("dom")
    a, c = shot // 2, shot % 2
    b, y = dom // 2, dom % 2
    same = c == y
    my_shot = 2 * a + y
    my_dom = 2 * b + c
    partner = (2 * a + y, 2 * b + c)

    barrier = pltpu.get_barrier_semaphore()

    def greet(shot_to, dom_to):
        pl.semaphore_signal(barrier, inc=1, device_id=(shot_to, dom_to), device_id_type=MESH)

    def greet_dom(i, carry):
        to = (dom + i) % n_dom
        greet(2 * a + c, to)
        greet(2 * a + 1 - c, to)
        return carry

    lax.fori_loop(1, n_dom, greet_dom, 0)
    greet(2 * a + 1 - c, dom)
    for i in range(1, groups):
        other = (a + i) % groups
        for cc in range(2):
            for yy in range(2):
                greet(2 * other + cc, 2 * b + yy)

    pl.semaphore_wait(barrier, 2 * n_dom - 1 + 4 * (groups - 1))

    def remote(src, dst, ssem, rsem, to):
        return pltpu.make_async_remote_copy(
            src_ref=src, dst_ref=dst, send_sem=ssem, recv_sem=rsem, device_id=to, device_id_type=MESH
        )

    def start_to(here, src, dst, ssem, rsem, to):
        @pl.when(here)
        def _():
            pltpu.make_async_copy(src, dst, rsem).start()

        @pl.when(jnp.logical_not(here))
        def _():
            remote(src, dst, ssem, rsem, to).start()

    def wait_sent(here, src, dst, ssem, rsem, to):
        @pl.when(jnp.logical_not(here))
        def _():
            remote(src, dst, ssem, rsem, to).wait_send()

    def wait_got(dst, rsem):
        pltpu.make_async_copy(dst, dst, rsem).wait()

    swaps = [
        (floats, floats_w),
        (ints, ints_w),
        (speed_in, speed),
        (now_in, lam.at[0]),
        (next_in, lam_next),
    ]

    def start_swap(i):
        start_to(same, swaps[i][0], swaps[i][1], swap_send.at[i], swap_recv.at[i], partner)

    def wait_swap(i):
        wait_got(swaps[i][1], swap_recv.at[i])

    start_swap(0)
    start_swap(1)

    def piece_to(o):
        here = jnp.logical_and(same, o == dom)
        return here, (2 * a + o % 2, 2 * (o // 2) + c)

    def send_piece(i, carry):
        o = (dom + i) % n_dom
        here, to = piece_to(o)
        send_buf[o] = parked[slot[o]]
        start_to(here, send_buf.at[o], recv_buf.at[dom], a2a_send.at[o], a2a_recv.at[dom], to)
        return carry

    lax.fori_loop(1, n_dom + 1, send_piece, 0)
    start_swap(2)
    start_swap(3)
    start_swap(4)

    row_i = lax.broadcasted_iota(jnp.int32, (lanes, lanes), 0)
    col_i = lax.broadcasted_iota(jnp.int32, (lanes, lanes), 1)
    apart = jnp.abs(row_i - col_i)
    matrix = jnp.zeros((lanes, lanes), F32)
    for k in range(1, 5):
        matrix = jnp.where(apart == k, stencil_coef[k], matrix)
    m_high, m_mid, m_low = split3(matrix)
    for i, part in enumerate((m_high, m_high, m_high, m_mid, m_mid, m_low)):
        band[i * lanes : (i + 1) * lanes, :] = part
    zeros_pad = jnp.zeros((depth, PAD, lanes), F32)
    for ch in range(2):
        e_buf[ch, :, 0:PAD, :] = zeros_pad
        e_buf[ch, :, PAD + width : 2 * PAD + width, :] = zeros_pad

    has_down = my_dom > 0
    has_up = my_dom < n_dom - 1
    top = 4 + depth

    @pl.when(jnp.logical_not(has_down))
    def _():
        def clear(i, carry):
            v_buf[i // STEPS, i % STEPS, 0:HALO] = jnp.zeros((HALO, width, lanes), F32)
            return carry

        lax.fori_loop(0, 2 * STEPS, clear, 0)

    @pl.when(jnp.logical_not(has_up))
    def _():
        def clear(i, carry):
            v_buf[i // STEPS, i % STEPS, top : top + HALO] = jnp.zeros((HALO, width, lanes), F32)
            return carry

        lax.fori_loop(0, 2 * STEPS, clear, 0)

    local_depth = rec_depth[...] - my_dom * depth
    rec_line = local_depth * width + rec_row[...] // lanes
    rec_lane = rec_row[...] % lanes
    wait_swap(0)
    wait_swap(1)
    to_scalar = pltpu.make_async_copy(ints_w, ints_s, local_sem)
    to_scalar.start()
    lane_hit = lax.broadcasted_iota(jnp.int32, (lanes, n_rec), 0) == rec_lane
    for k in range(STEPS):
        amounts = jnp.where(lane_hit, floats_w[k : k + 1, 0:n_rec], 0.0)
        for i, part in enumerate(split3(amounts)):
            parts[i, k * lanes : (k + 1) * lanes, :] = part
    to_scalar.wait()

    def inject_plane(z, carry):
        line = lax.broadcasted_iota(jnp.int32, (width, n_rec), 0) + z * width
        hit = jnp.where(line == rec_line, 1.0, 0.0).astype(BF16)
        total = jnp.zeros((width, STEPS * lanes), F32)
        for i in range(3):
            total = total + lax.dot_general(
                hit, parts[i], (((1,), (1,)), ((), ())), preferred_element_type=F32
            )
        for k in range(STEPS):
            inject[k, z] = total[:, k * lanes : (k + 1) * lanes]
        return carry

    lax.fori_loop(0, depth, inject_plane, 0)

    src_plane = ints_s[1, 0] - my_dom * depth
    cell = lax.broadcasted_iota(jnp.int32, (width, lanes), 0) * lanes + lax.broadcasted_iota(
        jnp.int32, (width, lanes), 1
    )
    src_mask[...] = jnp.where(cell == ints_s[1, 1], 1.0, 0.0)

    down = (2 * a + (my_dom - 1) % 2, 2 * ((my_dom + 1) // 2 - 1) + y)
    up = (2 * a + (my_dom + 1) % 2, 2 * ((my_dom + 1) // 2) + y)

    def to_down(ch, n):
        i = (ch * STEPS + n) * 2
        v = v_buf.at[ch, n]
        return remote(
            v.at[pl.ds(HALO, HALO)], v.at[pl.ds(top, HALO)], halo_send.at[i], halo_recv.at[i + 1], down
        )

    def to_up(ch, n):
        i = (ch * STEPS + n) * 2
        v = v_buf.at[ch, n]
        return remote(
            v.at[pl.ds(top - HALO, HALO)], v.at[pl.ds(0, HALO)], halo_send.at[i + 1], halo_recv.at[i], up
        )

    def send_down(ch, n):
        @pl.when(has_down)
        def _():
            to_down(ch, n).start()

    def send_up(ch, n):
        @pl.when(has_up)
        def _():
            to_up(ch, n).start()

    def wait_halo(ch, n):
        i = (ch * STEPS + n) * 2
        v = v_buf.at[ch, n]

        @pl.when(has_down)
        def _():
            wait_got(v.at[pl.ds(0, HALO)], halo_recv.at[i])

        @pl.when(has_up)
        def _():
            wait_got(v.at[pl.ds(top, HALO)], halo_recv.at[i + 1])

    def put_field(ch, n, z, value):
        v_buf[ch, n, z + HALO] = value
        e_buf[ch, z, PAD : PAD + width, :] = value

    def lateral(ch, dst):
        def plane(z, carry):
            mid_rows = e_buf[ch, z, PAD : PAD + width, :]
            high, mid, low = split3(mid_rows)
            lhs = jnp.concatenate([high, mid, low, high, mid, high], axis=1)
            total = jnp.dot(lhs, band[...], preferred_element_type=F32)
            total = total + 3.0 * stencil_coef[0] * mid_rows
            for k in range(1, 5):
                total = total + stencil_coef[k] * (
                    e_buf[ch, z, PAD + k : PAD + k + width, :] + e_buf[ch, z, PAD - k : PAD - k + width, :]
                )
            dst[z] = total
            return carry

        lax.fori_loop(0, depth, plane, 0, unroll=2)

    def vertical(ch, n, z):
        total = stencil_coef[1] * (v_buf[ch, n, z + HALO + 1] + v_buf[ch, n, z + HALO - 1])
        for k in range(2, 5):
            total = total + stencil_coef[k] * (v_buf[ch, n, z + HALO + k] + v_buf[ch, n, z + HALO - k])
        return total

    def sweep(body, ch, n):
        lax.fori_loop(0, HALO, body, 0)
        if n is not None:
            send_down(ch, n)
        lax.fori_loop(HALO, depth, body, 0)
        if n is not None:
            send_up(ch, n)

    for h in range(n_dom):
        wait_got(recv_buf.at[h], a2a_recv.at[h])
    rows = recv_buf.shape[1]
    half = n_dom // 2
    per = max(1, rows // width)
    cut = min(rows, width)

    def unpack(p, carry):
        older = recv_buf[ints_s[0, p]].astype(F32)
        newer = recv_buf[ints_s[0, p + half]].astype(F32)
        if rows >= width:
            for j in range(per):
                u_first[p * per + j] = older[j * width : (j + 1) * width]
                put_field(0, 0, p * per + j, newer[j * width : (j + 1) * width])
        else:
            parts_of = width // cut
            z, at = p // parts_of, (p % parts_of) * cut
            at = pl.multiple_of(at, cut)
            u_first[z, pl.ds(at, cut), :] = older
            v_buf[0, 0, z + HALO, pl.ds(at, cut), :] = newer
            e_buf[0, z, pl.ds(at + PAD, cut), :] = newer
        return carry

    lax.fori_loop(0, half, unpack, 0)
    send_down(0, 0)
    send_up(0, 0)
    lateral(0, lap.at[0])

    wait_swap(2)
    wait_swap(3)

    def first_scaled(z, carry):
        put_field(1, 0, z, speed[z] * lam[0, z])
        return carry

    sweep(first_scaled, 1, 0)
    lateral(1, lap_adj)

    def start_late(i, src, dst):
        start_to(same, src, dst, swap_send.at[i], swap_recv.at[i], partner)

    lam_next_ready = False
    for n in range(STEPS):
        wait_halo(0, n)
        last = n == STEPS - 1

        def forward(z, carry, n=n, last=last):
            value = lap[n, z] + vertical(0, n, z)
            lap[n, z] = value
            if not last:
                older = u_first[z] if n == 0 else v_buf[0, n - 1, z + HALO]
                amount = floats_w[n : n + 1, n_rec : n_rec + lanes] * jnp.where(src_plane == z, 1.0, 0.0)
                put_field(
                    0,
                    n + 1,
                    z,
                    2.0 * v_buf[0, n, z + HALO] - older + speed[z] * value + src_mask[...] * amount,
                )
            return carry

        sweep(forward, 0, None if last else n + 1)
        if not last:
            lateral(0, lap.at[n + 1])
        else:

            def gradient(z, carry):
                total = lam[0, z] * lap[STEPS - 1, z]
                for k in range(1, STEPS):
                    total = total + lam[k, z] * lap[STEPS - 1 - k, z]
                total = grad_scale * total
                for j in range(n_shot):
                    grad_send[j, z] = total[j * share : (j + 1) * share]
                return carry

            lax.fori_loop(0, depth, gradient, 0)
            for j in range(n_shot):
                start_to(
                    jnp.logical_and(same, shot == j),
                    grad_send.at[j],
                    grad_recv.at[my_shot],
                    grad_ssem.at[j],
                    grad_rsem.at[my_shot],
                    (j, 2 * b + c),
                )

        if not lam_next_ready:
            wait_swap(4)
            lam_next_ready = True
        wait_halo(1, n)

        def adjoint(z, carry, n=n, last=last):
            older = lam_next[z] if n == 0 else lam[n - 1, z]
            value = 2.0 * lam[n, z] - older + (lap_adj[z] + vertical(1, n, z)) + inject[n, z]
            if last:
                lam_out[z] = value
            else:
                lam[n + 1, z] = value
                put_field(1, n + 1, z, speed[z] * value)
            return carry

        sweep(adjoint, 1, None if last else n + 1)
        if n == STEPS - 2:
            start_late(5, lam.at[STEPS - 1], late_out)
        if last:
            start_late(6, lam_out, early_out)
        else:
            lateral(1, lap_adj)

    for j in range(n_shot):
        wait_got(grad_recv.at[j], grad_rsem.at[j])
    total = grad_recv[0]
    for j in range(1, n_shot):
        total = total + grad_recv[j]
    grad_out[...] = total
    wait_got(late_out, swap_recv.at[5])
    wait_got(early_out, swap_recv.at[6])

    for i, (src, dst) in enumerate(swaps + [(lam.at[STEPS - 1], late_out), (lam_out, early_out)]):
        wait_sent(same, src, dst, swap_send.at[i], swap_recv.at[i], partner)

    def piece_sent(o, carry):
        here, to = piece_to(o)
        wait_sent(here, send_buf.at[o], recv_buf.at[dom], a2a_send.at[o], a2a_recv.at[dom], to)
        return carry

    lax.fori_loop(0, n_dom, piece_sent, 0)
    for j in range(n_shot):
        wait_sent(
            jnp.logical_and(same, shot == j),
            grad_send.at[j],
            grad_recv.at[my_shot],
            grad_ssem.at[j],
            grad_rsem.at[my_shot],
            (j, 2 * b + c),
        )

    @pl.when(has_down)
    def _():
        for ch in range(2):
            for n in range(STEPS):
                to_down(ch, n).wait_send()

    @pl.when(has_up)
    def _():
        for ch in range(2):
            for n in range(STEPS):
                to_up(ch, n).wait_send()


def per_device(
    n_shot,
    n_dom,
    parked,
    parked_slot,
    holder_list,
    speed_sq,
    adjoint_next,
    adjoint_now,
    wavelet,
    src_depth,
    src_row,
    rec_depth,
    rec_row,
    residuals,
):
    depth, width, lanes = speed_sq.shape
    n_rec = rec_depth.shape[0]
    piece = parked.shape[2]
    rows = piece // lanes
    pieces = parked[0].reshape(n_dom, rows, lanes)
    ints = jnp.concatenate(
        [
            jnp.pad(holder_list[0], ((0, 0), (0, 128 - n_dom))),
            jnp.pad(jnp.concatenate([src_depth, src_row])[None], ((0, 6), (0, 126))),
        ],
        axis=0,
    )
    floats = jnp.concatenate(
        [
            jnp.pad(residuals[0], ((0, 8 - STEPS), (0, 0))),
            jnp.broadcast_to(
                jnp.pad(wavelet[0], (0, 8 - (STEPS - 1)))[:, None], (8, lanes)
            ),
        ],
        axis=1,
    )
    vmem = pl.BlockSpec(memory_space=pltpu.VMEM)
    smem = pl.BlockSpec(memory_space=pltpu.SMEM)
    slab = (depth, width, lanes)
    dma = pltpu.SemaphoreType.DMA
    share = width // n_shot
    grad, late, early = pl.pallas_call(
        functools.partial(window_kernel, n_shot, n_dom),
        out_shape=[
            jax.ShapeDtypeStruct((depth, share, lanes), F32),
            jax.ShapeDtypeStruct(slab, F32),
            jax.ShapeDtypeStruct(slab, F32),
        ],
        in_specs=[vmem, smem] + [vmem] * 7,
        out_specs=[vmem] * 3,
        scratch_shapes=[
            pltpu.VMEM((n_dom, rows, lanes), BF16),
            pltpu.VMEM((n_dom, rows, lanes), BF16),
            pltpu.VMEM((8, 128), jnp.int32),
            pltpu.SMEM((8, 128), jnp.int32),
            pltpu.VMEM((8, n_rec + lanes), F32),
            pltpu.VMEM(slab, F32),
            pltpu.VMEM(slab, F32),
            pltpu.VMEM((STEPS,) + slab, F32),
            pltpu.VMEM(slab, F32),
            pltpu.VMEM((2, STEPS, depth + 2 * HALO, width, lanes), F32),
            pltpu.VMEM((2, depth, width + 2 * PAD, lanes), F32),
            pltpu.VMEM((STEPS,) + slab, F32),
            pltpu.VMEM(slab, F32),
            pltpu.VMEM((6 * lanes, lanes), BF16),
            pltpu.VMEM((3, STEPS * lanes, n_rec), BF16),
            pltpu.VMEM((STEPS,) + slab, F32),
            pltpu.VMEM((width, lanes), F32),
            pltpu.VMEM((n_shot, depth, share, lanes), F32),
            pltpu.VMEM((n_shot, depth, share, lanes), F32),
            pltpu.VMEM(slab, F32),
            dma((n_dom,)),
            dma((n_dom,)),
            dma((7,)),
            dma((7,)),
            dma((4 * STEPS,)),
            dma((4 * STEPS,)),
            dma((n_shot,)),
            dma((n_shot,)),
            dma,
        ],
        compiler_params=pltpu.CompilerParams(
            collective_id=0, has_side_effects=True, vmem_limit_bytes=48 * 1024 * 1024
        ),
        name="adjoint_window",
    )(
        pieces,
        parked_slot[0, 0],
        ints,
        speed_sq,
        adjoint_next[0],
        adjoint_now[0],
        floats,
        rec_depth[None],
        rec_row[None],
    )
    return grad, late[None], early[None]


def solution(mesh):
    n_shot, n_dom = mesh.shape["shot"], mesh.shape["dom"]
    in_specs = (
        P("shot", "dom", None),
        P("shot", "dom", None),
        P("shot", "dom", None),
        P("dom", None, None),
        P("shot", "dom", None, None),
        P("shot", "dom", None, None),
        P("shot", None),
        P("shot"),
        P("shot"),
        P(),
        P(),
        P("shot", None, None),
    )
    out_specs = (P("dom", "shot", None), P("shot", "dom", None, None), P("shot", "dom", None, None))
    return jax.shard_map(
        functools.partial(per_device, n_shot, n_dom),
        mesh=mesh,
        in_specs=in_specs,
        out_specs=out_specs,
        check_vma=False,
    )
```

time: 196 us -> 69 us (0.35)
  the two profiles are of different devices: /device:TPU:0 before, /device:TPU:11 now
where the time goes in v1:
time: 69 us; the launch traced here: 68.8 us
  Pallas kernels  60.2 us (87%)
  local copies, waits for them, and re-layouts  6.48 us (9%)
  between operations  2.03 us (3%)
    pallas_call x1, Pallas kernels, per_device(): pl.pallas_call(functools.partial(window_kernel, n_shot, n_dom), out_shape...  60.2 us
    unnamed x22, local copies, waits for them, and re-layouts  6.4 us

profile of v1, /device:TPU:11, one launch (start us, length us, event | category | flops | bytes accessed | tf_op | source)
XLA Modules:
  0.0 68.8 jit_solution(8419611724168573685)
XLA Ops:
  1.3 0.0 copy-start.6
  1.9 0.1 add_bitcast_fusion
  2.0 0.0 copy-start.8
  2.0 0.7 copy-done.8
  2.7 0.0 copy-start.7
  2.7 0.1 broadcast_in_dim.22
  2.8 0.6 copy-done.7
  3.3 0.0 copy-done.6
  3.3 0.0 copy-start.3
  3.4 0.0 copy-start.4
  3.4 0.0 copy-start
  3.4 0.0 copy-start.1
  3.4 1.2 %copy.17 = bf16[1,8,256,128]{3,2,1,0:T(8,128)(2,1)S(1)} copy(bf16[1,8,256,128]{3,1,2,0:T(8,128)(2,1)} %bitcast.25) | data formatting | bytes 1048576
  4.6 0.0 copy-start.5
  4.6 0.0 copy-done.3
  4.6 0.0 copy-done.4
  4.6 0.0 copy-done
  4.7 0.1 copy-done.1
  4.7 0.6 copy-done.5
  5.3 1.0 %copy-done.2 = f32[1,8,128,128]{3,2,1,0:T(8,128)S(1)} copy-done((f32[1,8,128,128]{3,2,1,0:T(8,128)S(1)}, f32[1,8,128,128]{3,2,1,0:T(8,128)}, u32[]{:S(2)}) %copy-start.2) | copy-done | bytes 524312
  6.3 60.2 %adjoint_window.1 = (f32[8,32,128]{2,1,0:T(8,128)S(1)}, f32[8,128,128]{2,1,0:T(8,128)S(1)}, f32[8,128,128]{2,1,0:T(8,128)S(1)}) custom-call(bf16[8,256,128]{2,1,0:T(8,128)(2,1)S(1)} %bitcast.17, s32[8]{0:T(128)S(1)} %bitcast.24, s32[8,128]{1,0:T(8,128)S(1)} %pad_add_fusion.ints, f32[8,128,128]{2,1,0:T(8,128)S(1)} %copy-done, f32[8,128,128]{2,1,0:T(8,128)S(1)} %bitcast.18, ...), custom_call_target="tpu_custom_call" | custom-call | tf_op jit(solution)/shard_map/adjoint_window/pallas_call | solution.py:496
  66.5 0.7 copy.23
  67.2 0.8 %copy.24 = f32[1,8,128,128]{3,2,1,0:T(8,128)} copy(f32[1,8,128,128]{3,2,1,0:T(8,128)S(1)} %bitcast.21) | data formatting | bytes 1048576
  68.0 0.8 %copy.25 = f32[1,8,128,128]{3,2,1,0:T(8,128)} copy(f32[1,8,128,128]{3,2,1,0:T(8,128)S(1)} %bitcast.20) | data formatting | bytes 1048576
  (4 shorter events, 0.0 us)
Async XLA Ops:
  1.3 2.1 %copy-start.6 = (f32[1,4,1024]{2,1,0:T(4,128)S(1)}, f32[1,4,1024]{2,1,0:T(4,128)}, u32[]{:S(2)}) copy-start(f32[1,4,1024]{2,1,0:T(4,128)} %param.23) | copy-start | bytes 49156
  2.0 0.7 copy-start.8
  2.7 0.7 copy-start.7
  3.3 1.3 %copy-start.3 = (s32[1024]{0:T(1024)S(1)}, s32[1024]{0:T(1024)}, u32[]{:S(2)}) copy-start(s32[1024]{0:T(1024)} %param.21) | copy-start | bytes 12292
  3.4 1.3 %copy-start.4 = (s32[1024]{0:T(1024)S(1)}, s32[1024]{0:T(1024)}, u32[]{:S(2)}) copy-start(s32[1024]{0:T(1024)} %param.22) | copy-start | bytes 12292
  3.4 1.3 %copy-start = (f32[8,128,128]{2,1,0:T(8,128)S(1)}, f32[8,128,128]{2,1,0:T(8,128)}, u32[]{:S(2)}) copy-start(f32[8,128,128]{2,1,0:T(8,128)} %speed_in.1) | copy-start | bytes 1572868
  3.4 1.4 %copy-start.1 = (f32[1,8,128,128]{3,2,1,0:T(8,128)S(1)}, f32[1,8,128,128]{3,2,1,0:T(8,128)}, u32[]{:S(2)}) copy-start(f32[1,8,128,128]{3,2,1,0:T(8,128)} %param.16) | copy-start | bytes 1572868
  4.6 0.7 %copy-start.5 = (s32[1,1,8]{2,1,0:T(1,128)S(1)}, s32[1,1,8]{2,1,0:T(1,128)}, u32[]{:S(2)}) copy-start(s32[1,1,8]{2,1,0:T(1,128)} %param.13) | copy-start | bytes 100
  5.3 1.0 %copy-start.2 = (f32[1,8,128,128]{3,2,1,0:T(8,128)S(1)}, f32[1,8,128,128]{3,2,1,0:T(8,128)}, u32[]{:S(2)}) copy-start(f32[1,8,128,128]{3,2,1,0:T(8,128)} %param.17) | copy-start | bytes 1572868

commit v2 on v1

--- a/solution.py
+++ b/solution.py
@@ -10,6 +10,7 @@
 STEPS = 4
 HALO = 4
 PAD = 8
+VMEM_BYTES = 56 * 1024 * 1024
 
 stencil_coef = (-205.0 / 72.0, 8.0 / 5.0, -1.0 / 5.0, 8.0 / 315.0, -1.0 / 560.0)
 grad_scale = 0.0625
@@ -62,6 +63,9 @@
     grad_send,
     grad_recv,
     lam_out,
+    lap_w,
+    grad_part,
+    grad_part_w,
     a2a_send,
     a2a_recv,
     swap_send,
@@ -81,7 +85,6 @@
     a, c = shot // 2, shot % 2
     b, y = dom // 2, dom % 2
     same = c == y
-    my_shot = 2 * a + y
     my_dom = 2 * b + c
     partner = (2 * a + y, 2 * b + c)
 
@@ -134,6 +137,10 @@
         (speed_in, speed),
         (now_in, lam.at[0]),
         (next_in, lam_next),
+        (lam.at[STEPS - 1], late_out),
+        (lam_out, early_out),
+        (lap.at[0], lap_w),
+        (grad_part, grad_part_w),
     ]
 
     def start_swap(i):
@@ -330,25 +337,11 @@
     send_up(0, 0)
     lateral(0, lap.at[0])
 
-    wait_swap(2)
-    wait_swap(3)
-
-    def first_scaled(z, carry):
-        put_field(1, 0, z, speed[z] * lam[0, z])
-        return carry
-
-    sweep(first_scaled, 1, 0)
-    lateral(1, lap_adj)
-
-    def start_late(i, src, dst):
-        start_to(same, src, dst, swap_send.at[i], swap_recv.at[i], partner)
-
-    lam_next_ready = False
-    for n in range(STEPS):
+    def forward_step(n):
+        last = n == STEPS - 1
         wait_halo(0, n)
-        last = n == STEPS - 1
-
-        def forward(z, carry, n=n, last=last):
+
+        def plane(z, carry):
             value = lap[n, z] + vertical(0, n, z)
             lap[n, z] = value
             if not last:
@@ -362,37 +355,15 @@
                 )
             return carry
 
-        sweep(forward, 0, None if last else n + 1)
+        sweep(plane, 0, None if last else n + 1)
         if not last:
             lateral(0, lap.at[n + 1])
-        else:
-
-            def gradient(z, carry):
-                total = lam[0, z] * lap[STEPS - 1, z]
-                for k in range(1, STEPS):
-                    total = total + lam[k, z] * lap[STEPS - 1 - k, z]
-                total = grad_scale * total
-                for j in range(n_shot):
-                    grad_send[j, z] = total[j * share : (j + 1) * share]
-                return carry
-
-            lax.fori_loop(0, depth, gradient, 0)
-            for j in range(n_shot):
-                start_to(
-                    jnp.logical_and(same, shot == j),
-                    grad_send.at[j],
-                    grad_recv.at[my_shot],
-                    grad_ssem.at[j],
-                    grad_rsem.at[my_shot],
-                    (j, 2 * b + c),
-                )
-
-        if not lam_next_ready:
-            wait_swap(4)
-            lam_next_ready = True
+
+    def adjoint_step(n):
+        last = n == STEPS - 1
         wait_halo(1, n)
 
-        def adjoint(z, carry, n=n, last=last):
+        def plane(z, carry):
             older = lam_next[z] if n == 0 else lam[n - 1, z]
             value = 2.0 * lam[n, z] - older + (lap_adj[z] + vertical(1, n, z)) + inject[n, z]
             if last:
@@ -402,24 +373,70 @@
                 put_field(1, n + 1, z, speed[z] * value)
             return carry
 
-        sweep(adjoint, 1, None if last else n + 1)
-        if n == STEPS - 2:
-            start_late(5, lam.at[STEPS - 1], late_out)
-        if last:
-            start_late(6, lam_out, early_out)
-        else:
-            lateral(1, lap_adj)
-
-    for j in range(n_shot):
+        sweep(plane, 1, None if last else n + 1)
+
+    wait_swap(2)
+    forward_step(0)
+    wait_swap(3)
+
+    def first_scaled(z, carry):
+        put_field(1, 0, z, speed[z] * lam[0, z])
+        return carry
+
+    sweep(first_scaled, 1, 0)
+    lateral(1, lap_adj)
+    forward_step(1)
+    wait_swap(4)
+    start_swap(7)
+    adjoint_step(0)
+    lateral(1, lap_adj)
+    forward_step(2)
+    adjoint_step(1)
+    lateral(1, lap_adj)
+    forward_step(3)
+
+    def early_terms(z, carry):
+        total = lam[0, z] * lap[STEPS - 1, z]
+        for k in range(1, STEPS - 1):
+            total = total + lam[k, z] * lap[STEPS - 1 - k, z]
+        grad_part[z] = total
+        return carry
+
+    lax.fori_loop(0, depth, early_terms, 0)
+    start_swap(8)
+    adjoint_step(2)
+    start_swap(5)
+    lateral(1, lap_adj)
+    adjoint_step(3)
+    start_swap(6)
+
+    wait_swap(7)
+    wait_swap(8)
+    wait_swap(5)
+
+    def gradient(z, carry):
+        total = grad_scale * (grad_part_w[z] + late_out[z] * lap_w[z])
+        for j in range(n_shot):
+            grad_send[j, z] = total[j * share : (j + 1) * share]
+        return carry
+
+    lax.fori_loop(0, depth, gradient, 0)
+
+    def share_to(i):
+        j = (shot + i) % n_shot
+        return remote(grad_send.at[j], grad_recv.at[shot], grad_ssem.at[j], grad_rsem.at[shot], (j, dom))
+
+    for i in range(1, n_shot):
+        share_to(i).start()
+    total = grad_send[shot]
+    for i in range(1, n_shot):
+        j = (shot + i) % n_shot
         wait_got(grad_recv.at[j], grad_rsem.at[j])
-    total = grad_recv[0]
-    for j in range(1, n_shot):
         total = total + grad_recv[j]
     grad_out[...] = total
-    wait_got(late_out, swap_recv.at[5])
-    wait_got(early_out, swap_recv.at[6])
-
-    for i, (src, dst) in enumerate(swaps + [(lam.at[STEPS - 1], late_out), (lam_out, early_out)]):
+    wait_swap(6)
+
+    for i, (src, dst) in enumerate(swaps):
         wait_sent(same, src, dst, swap_send.at[i], swap_recv.at[i], partner)
 
     def piece_sent(o, carry):
@@ -428,15 +445,8 @@
         return carry
 
     lax.fori_loop(0, n_dom, piece_sent, 0)
-    for j in range(n_shot):
-        wait_sent(
-            jnp.logical_and(same, shot == j),
-            grad_send.at[j],
-            grad_recv.at[my_shot],
-            grad_ssem.at[j],
-            grad_rsem.at[my_shot],
-            (j, 2 * b + c),
-        )
+    for i in range(1, n_shot):
+        share_to(i).wait_send()
 
     @pl.when(has_down)
     def _():
@@ -449,6 +459,15 @@
         for ch in range(2):
             for n in range(STEPS):
                 to_up(ch, n).wait_send()
+
+
+def hand_on(*refs):
+    sems = refs[6]
+    copies = [pltpu.make_async_copy(refs[i], refs[3 + i], sems.at[i]) for i in range(3)]
+    for copy in copies:
+        copy.start()
+    for copy in copies:
+        copy.wait()
 
 
 def per_device(
@@ -490,6 +509,7 @@
     )
     vmem = pl.BlockSpec(memory_space=pltpu.VMEM)
     smem = pl.BlockSpec(memory_space=pltpu.SMEM)
+    anywhere = pl.BlockSpec(memory_space=pl.ANY)
     slab = (depth, width, lanes)
     dma = pltpu.SemaphoreType.DMA
     share = width // n_shot
@@ -500,7 +520,7 @@
             jax.ShapeDtypeStruct(slab, F32),
             jax.ShapeDtypeStruct(slab, F32),
         ],
-        in_specs=[vmem, smem] + [vmem] * 7,
+        in_specs=[vmem, smem, vmem, anywhere, anywhere, anywhere] + [vmem] * 3,
         out_specs=[vmem] * 3,
         scratch_shapes=[
             pltpu.VMEM((n_dom, rows, lanes), BF16),
@@ -523,10 +543,13 @@
             pltpu.VMEM((n_shot, depth, share, lanes), F32),
             pltpu.VMEM((n_shot, depth, share, lanes), F32),
             pltpu.VMEM(slab, F32),
+            pltpu.VMEM(slab, F32),
+            pltpu.VMEM(slab, F32),
+            pltpu.VMEM(slab, F32),
             dma((n_dom,)),
             dma((n_dom,)),
-            dma((7,)),
-            dma((7,)),
+            dma((9,)),
+            dma((9,)),
             dma((4 * STEPS,)),
             dma((4 * STEPS,)),
             dma((n_shot,)),
@@ -534,7 +557,7 @@
             dma,
         ],
         compiler_params=pltpu.CompilerParams(
-            collective_id=0, has_side_effects=True, vmem_limit_bytes=48 * 1024 * 1024
+            collective_id=0, has_side_effects=True, vmem_limit_bytes=VMEM_BYTES
         ),
         name="adjoint_window",
     )(
@@ -548,6 +571,15 @@
         rec_depth[None],
         rec_row[None],
     )
+    outs = (grad, late, early)
+    grad, late, early = pl.pallas_call(
+        hand_on,
+        out_shape=[jax.ShapeDtypeStruct(x.shape, x.dtype) for x in outs],
+        in_specs=[anywhere] * 3,
+        out_specs=[anywhere] * 3,
+        scratch_shapes=[dma((3,))],
+        name="hand_on",
+    )(*outs)
     return grad, late[None], early[None]
 
 

time: 69 us -> 104 us (1.51)
  Pallas kernels: 60.2 us -> 97.5 us
  local copies, waits for them, and re-layouts: 6.48 us -> 3.22 us
  other arithmetic: 0.09 us -> 1.29 us
    pallas_call x0 -> x1, Pallas kernels: none -> 36.9 us  [per_device(): pl.pallas_call(hand_on, out_shape=[jax.ShapeDtypeStruct(x.shape, x.dtype)...]
    unnamed x22 -> x7, local copies, waits for them, and re-layouts: 6.4 us -> 3.15 us
where the time goes in v2:
time: 104 us
  Pallas kernels  97.5 us (94%)
  local copies, waits for them, and re-layouts  3.22 us (3%)
  between operations  1.96 us (2%)
  other arithmetic  1.29 us (1%)
    pallas_call x1, Pallas kernels, per_device(): pl.pallas_call(functools.partial(window_kernel, n_shot, n_dom), out_shape...  60.7 us
    pallas_call x1, Pallas kernels, per_device(): pl.pallas_call(hand_on, out_shape=[jax.ShapeDtypeStruct(x.shape, x.dtype)...  36.9 us
    unnamed x7, local copies, waits for them, and re-layouts  3.15 us

profile of v2, /device:TPU:11, one launch (start us, length us, event | category | flops | bytes accessed | tf_op | source)
XLA Modules:
  0.0 104.0 jit_solution(10777568851971939301)
XLA Ops:
  1.3 0.0 copy-start
  1.9 0.1 add_bitcast_fusion
  2.0 0.0 copy-start.2
  2.0 0.7 copy-done.2
  2.7 0.0 copy-start.1
  2.7 0.1 broadcast_in_dim.22
  2.8 0.6 copy-done.1
  3.3 0.6 pad_add_fusion.ints
  3.9 0.0 copy-done
  3.9 0.6 select_maximum_fusion.floats
  4.6 1.9 %copy.17 = bf16[1,8,256,128]{3,2,1,0:T(8,128)(2,1)} copy(bf16[1,8,256,128]{3,1,2,0:T(8,128)(2,1)} %bitcast.20) | data formatting | bytes 1048576
  6.5 60.7 %adjoint_window.1 = (f32[8,32,128]{2,1,0:T(8,128)}, f32[8,128,128]{2,1,0:T(8,128)}, f32[8,128,128]{2,1,0:T(8,128)}) custom-call(bf16[8,256,128]{2,1,0:T(8,128)(2,1)} %bitcast.17, s32[8]{0:T(128)} %bitcast.24, s32[8,128]{1,0:T(8,128)} %pad_add_fusion.ints, f32[8,128,128]{2,1,0:T(8,128)} %speed_in.1, f32[8,128,128]{2,1,0:T(8,128)} %bitcast.18, ...), custom_call_target="tpu_custom_call" | custom-call | tf_op jit(solution)/shard_map/adjoint_window/pallas_call | solution.py:516
  67.1 36.9 %hand_on.1 = (f32[8,32,128]{2,1,0:T(8,128)}, f32[8,128,128]{2,1,0:T(8,128)}, f32[8,128,128]{2,1,0:T(8,128)}) custom-call(f32[8,32,128]{2,1,0:T(8,128)} %get-tuple-element.9.refs_0_, f32[8,128,128]{2,1,0:T(8,128)} %get-tuple-element.10.refs_1_, f32[8,128,128]{2,1,0:T(8,128)} %get-tuple-element.11.refs_2_), custom_call_target="tpu_custom_call" | custom-call | tf_op jit(solution)/shard_map/hand_on/pallas_call | solution.py:575
  (1 shorter events, 0.0 us)
Async XLA Ops:
  1.3 2.7 %copy-start = (f32[1,4,1024]{2,1,0:T(4,128)S(1)}, f32[1,4,1024]{2,1,0:T(4,128)}, u32[]{:S(2)}) copy-start(f32[1,4,1024]{2,1,0:T(4,128)} %param.23) | copy-start | bytes 49156
  2.0 0.7 copy-start.2
  2.7 0.7 copy-start.1

commit v3 on v2

--- a/solution.py
+++ b/solution.py
@@ -20,12 +20,9 @@
 BF16 = jnp.bfloat16
 
 
-def split3(value):
+def split2(value):
     high = value.astype(BF16)
-    rest = value - high.astype(F32)
-    mid = rest.astype(BF16)
-    low = (rest - mid.astype(F32)).astype(BF16)
-    return high, mid, low
+    return high, (value - high.astype(F32)).astype(BF16)
 
 
 def window_kernel(
@@ -33,11 +30,14 @@
     n_dom,
     parked,
     slot,
-    ints,
+    holder,
+    wavelet,
+    src_depth,
+    src_row,
+    residuals,
     speed_in,
     next_in,
     now_in,
-    floats,
     rec_depth,
     rec_row,
     grad_out,
@@ -45,6 +45,8 @@
     early_out,
     send_buf,
     recv_buf,
+    ints,
+    floats,
     ints_w,
     ints_s,
     floats_w,
@@ -88,6 +90,19 @@
     my_dom = 2 * b + c
     partner = (2 * a + y, 2 * b + c)
 
+    lane = lax.broadcasted_iota(jnp.int32, (8, 128), 1)
+    line = lax.broadcasted_iota(jnp.int32, (8, 128), 0)
+    first = lax.fori_loop(
+        0, n_dom, lambda p, v: jnp.where(lane == p, holder[p], v), jnp.zeros((8, 128), jnp.int32)
+    )
+    second = jnp.where(lane == 0, src_depth[0], src_row[0])
+    ints[...] = jnp.where(line == 0, first, second)
+    floats[0:STEPS, 0:n_rec] = residuals[...]
+    for n in range(STEPS - 1):
+        floats[n : n + 1, n_rec : n_rec + lanes] = jnp.full((1, lanes), wavelet[n], F32)
+    floats[STEPS - 1 : STEPS, n_rec : n_rec + lanes] = jnp.zeros((1, lanes), F32)
+    floats[STEPS:8, :] = jnp.zeros((8 - STEPS, n_rec + lanes), F32)
+
     barrier = pltpu.get_barrier_semaphore()
 
     def greet(shot_to, dom_to):
@@ -165,8 +180,6 @@
 
     lax.fori_loop(1, n_dom + 1, send_piece, 0)
     start_swap(2)
-    start_swap(3)
-    start_swap(4)
 
     row_i = lax.broadcasted_iota(jnp.int32, (lanes, lanes), 0)
     col_i = lax.broadcasted_iota(jnp.int32, (lanes, lanes), 1)
@@ -174,8 +187,8 @@
     matrix = jnp.zeros((lanes, lanes), F32)
     for k in range(1, 5):
         matrix = jnp.where(apart == k, stencil_coef[k], matrix)
-    m_high, m_mid, m_low = split3(matrix)
-    for i, part in enumerate((m_high, m_high, m_high, m_mid, m_mid, m_low)):
+    m_high, m_low = split2(matrix)
+    for i, part in enumerate((m_high, m_high, m_low, m_low)):
         band[i * lanes : (i + 1) * lanes, :] = part
     zeros_pad = jnp.zeros((depth, PAD, lanes), F32)
     for ch in range(2):
@@ -212,24 +225,28 @@
     lane_hit = lax.broadcasted_iota(jnp.int32, (lanes, n_rec), 0) == rec_lane
     for k in range(STEPS):
         amounts = jnp.where(lane_hit, floats_w[k : k + 1, 0:n_rec], 0.0)
-        for i, part in enumerate(split3(amounts)):
+        for i, part in enumerate(split2(amounts)):
             parts[i, k * lanes : (k + 1) * lanes, :] = part
     to_scalar.wait()
 
-    def inject_plane(z, carry):
-        line = lax.broadcasted_iota(jnp.int32, (width, n_rec), 0) + z * width
+    group = depth // 2
+
+    def inject_half(h, carry):
+        line = lax.broadcasted_iota(jnp.int32, (group * width, n_rec), 0) + h * (group * width)
         hit = jnp.where(line == rec_line, 1.0, 0.0).astype(BF16)
-        total = jnp.zeros((width, STEPS * lanes), F32)
-        for i in range(3):
+        total = jnp.zeros((group * width, STEPS * lanes), F32)
+        for i in range(2):
             total = total + lax.dot_general(
                 hit, parts[i], (((1,), (1,)), ((), ())), preferred_element_type=F32
             )
         for k in range(STEPS):
-            inject[k, z] = total[:, k * lanes : (k + 1) * lanes]
-        return carry
-
-    lax.fori_loop(0, depth, inject_plane, 0)
-
+            for z in range(group):
+                inject[k, h * group + z] = total[z * width : (z + 1) * width, k * lanes : (k + 1) * lanes]
+        return carry
+
+    lax.fori_loop(0, 2, inject_half, 0)
+
+    start_swap(3)
     src_plane = ints_s[1, 0] - my_dom * depth
     cell = lax.broadcasted_iota(jnp.int32, (width, lanes), 0) * lanes + lax.broadcasted_iota(
         jnp.int32, (width, lanes), 1
@@ -280,20 +297,24 @@
         e_buf[ch, z, PAD : PAD + width, :] = value
 
     def lateral(ch, dst):
-        def plane(z, carry):
-            mid_rows = e_buf[ch, z, PAD : PAD + width, :]
-            high, mid, low = split3(mid_rows)
-            lhs = jnp.concatenate([high, mid, low, high, mid, high], axis=1)
-            total = jnp.dot(lhs, band[...], preferred_element_type=F32)
-            total = total + 3.0 * stencil_coef[0] * mid_rows
-            for k in range(1, 5):
-                total = total + stencil_coef[k] * (
-                    e_buf[ch, z, PAD + k : PAD + k + width, :] + e_buf[ch, z, PAD - k : PAD - k + width, :]
-                )
-            dst[z] = total
+        def planes(h, carry):
+            z = h * group
+            own = e_buf[ch, pl.ds(z, group), PAD : PAD + width, :]
+            high, low = split2(own.reshape(group * width, lanes))
+            total = jnp.dot(
+                jnp.concatenate([high, low, high, low], axis=1), band[...], preferred_element_type=F32
+            ).reshape(group, width, lanes)
+            for p in range(group):
+                value = total[p] + 3.0 * stencil_coef[0] * own[p]
+                for k in range(1, 5):
+                    value = value + stencil_coef[k] * (
+                        e_buf[ch, z + p, PAD + k : PAD + k + width, :]
+                        + e_buf[ch, z + p, PAD - k : PAD - k + width, :]
+                    )
+                dst[z + p] = value
             return carry
 
-        lax.fori_loop(0, depth, plane, 0, unroll=2)
+        lax.fori_loop(0, 2, planes, 0)
 
     def vertical(ch, n, z):
         total = stencil_coef[1] * (v_buf[ch, n, z + HALO + 1] + v_buf[ch, n, z + HALO - 1])
@@ -311,6 +332,7 @@
 
     for h in range(n_dom):
         wait_got(recv_buf.at[h], a2a_recv.at[h])
+    start_swap(4)
     rows = recv_buf.shape[1]
     half = n_dom // 2
     per = max(1, rows // width)
@@ -459,15 +481,6 @@
         for ch in range(2):
             for n in range(STEPS):
                 to_up(ch, n).wait_send()
-
-
-def hand_on(*refs):
-    sems = refs[6]
-    copies = [pltpu.make_async_copy(refs[i], refs[3 + i], sems.at[i]) for i in range(3)]
-    for copy in copies:
-        copy.start()
-    for copy in copies:
-        copy.wait()
 
 
 def per_device(
@@ -491,22 +504,6 @@
     piece = parked.shape[2]
     rows = piece // lanes
     pieces = parked[0].reshape(n_dom, rows, lanes)
-    ints = jnp.concatenate(
-        [
-            jnp.pad(holder_list[0], ((0, 0), (0, 128 - n_dom))),
-            jnp.pad(jnp.concatenate([src_depth, src_row])[None], ((0, 6), (0, 126))),
-        ],
-        axis=0,
-    )
-    floats = jnp.concatenate(
-        [
-            jnp.pad(residuals[0], ((0, 8 - STEPS), (0, 0))),
-            jnp.broadcast_to(
-                jnp.pad(wavelet[0], (0, 8 - (STEPS - 1)))[:, None], (8, lanes)
-            ),
-        ],
-        axis=1,
-    )
     vmem = pl.BlockSpec(memory_space=pltpu.VMEM)
     smem = pl.BlockSpec(memory_space=pltpu.SMEM)
     anywhere = pl.BlockSpec(memory_space=pl.ANY)
@@ -520,12 +517,14 @@
             jax.ShapeDtypeStruct(slab, F32),
             jax.ShapeDtypeStruct(slab, F32),
         ],
-        in_specs=[vmem, smem, vmem, anywhere, anywhere, anywhere] + [vmem] * 3,
+        in_specs=[vmem] + [smem] * 5 + [vmem] + [anywhere] * 3 + [vmem] * 2,
         out_specs=[vmem] * 3,
         scratch_shapes=[
             pltpu.VMEM((n_dom, rows, lanes), BF16),
             pltpu.VMEM((n_dom, rows, lanes), BF16),
             pltpu.VMEM((8, 128), jnp.int32),
+            pltpu.VMEM((8, n_rec + lanes), F32),
+            pltpu.VMEM((8, 128), jnp.int32),
             pltpu.SMEM((8, 128), jnp.int32),
             pltpu.VMEM((8, n_rec + lanes), F32),
             pltpu.VMEM(slab, F32),
@@ -536,8 +535,8 @@
             pltpu.VMEM((2, depth, width + 2 * PAD, lanes), F32),
             pltpu.VMEM((STEPS,) + slab, F32),
             pltpu.VMEM(slab, F32),
-            pltpu.VMEM((6 * lanes, lanes), BF16),
-            pltpu.VMEM((3, STEPS * lanes, n_rec), BF16),
+            pltpu.VMEM((4 * lanes, lanes), BF16),
+            pltpu.VMEM((2, STEPS * lanes, n_rec), BF16),
             pltpu.VMEM((STEPS,) + slab, F32),
             pltpu.VMEM((width, lanes), F32),
             pltpu.VMEM((n_shot, depth, share, lanes), F32),
@@ -563,23 +562,17 @@
     )(
         pieces,
         parked_slot[0, 0],
-        ints,
+        holder_list[0, 0],
+        wavelet[0],
+        src_depth,
+        src_row,
+        residuals[0],
         speed_sq,
         adjoint_next[0],
         adjoint_now[0],
-        floats,
         rec_depth[None],
         rec_row[None],
     )
-    outs = (grad, late, early)
-    grad, late, early = pl.pallas_call(
-        hand_on,
-        out_shape=[jax.ShapeDtypeStruct(x.shape, x.dtype) for x in outs],
-        in_specs=[anywhere] * 3,
-        out_specs=[anywhere] * 3,
-        scratch_shapes=[dma((3,))],
-        name="hand_on",
-    )(*outs)
     return grad, late[None], early[None]
 
 

time: 104 us -> 68.7 us (0.66)
  Pallas kernels: 97.5 us -> 60.2 us
  local copies, waits for them, and re-layouts: 3.22 us -> 6.2 us
  other arithmetic: 1.29 us -> 0 us
    pallas_call x1 -> x0, Pallas kernels: 36.9 us -> none  [per_device(): pl.pallas_call(hand_on, out_shape=[jax.ShapeDtypeStruct(x.shape, x.dtype)...]
    unnamed x7 -> x6, local copies, waits for them, and re-layouts: 3.15 us -> 6.2 us
    concatenate x2 -> x0, other arithmetic: 1.22 us -> none  [the longest x1 0.62 us: per_device(): jnp.concatenate([jnp.pad(residuals[0], ((0, 8 - STEPS), (0, 0))), jnp.bro...]
where the time goes in v3:
time: 68.7 us; the launch traced here: 68.3 us
  Pallas kernels  60.2 us (88%)
  local copies, waits for them, and re-layouts  6.2 us (9%)
  between operations  1.93 us (3%)
    pallas_call x1, Pallas kernels, per_device(): pl.pallas_call(functools.partial(window_kernel, n_shot, n_dom), out_shape...  60.2 us
    unnamed x6, local copies, waits for them, and re-layouts  6.2 us

profile of v3, /device:TPU:11, one launch (start us, length us, event | category | flops | bytes accessed | tf_op | source)
XLA Modules:
  0.0 68.3 jit_solution(7018517685136323503)
XLA Ops:
  1.9 1.9 %copy.17 = bf16[1,8,256,128]{3,2,1,0:T(8,128)(2,1)} copy(bf16[1,8,256,128]{3,1,2,0:T(8,128)(2,1)} %bitcast.16) | data formatting | bytes 1048576
  3.8 60.2 %adjoint_window.1 = (f32[8,32,128]{2,1,0:T(8,128)}, f32[8,128,128]{2,1,0:T(8,128)}, f32[8,128,128]{2,1,0:T(8,128)}) custom-call(bf16[8,256,128]{2,1,0:T(8,128)(2,1)} %bitcast.15, s32[8]{0:T(128)} %bitcast.24, s32[8]{0:T(128)} %bitcast.25, f32[3]{0:T(128)} %bitcast.26, s32[1]{0:T(128)S(6)} %copy.21.src_depth, s32[1]{0:T(128)S(6)} %copy.22.src_row, ...), custom_call_target="tpu_custom_call" | custom-call | tf_op jit(solution)/shard_map/adjoint_window/pallas_call | solution.py:513
  64.0 1.6 %copy.23 = f32[8,32,128]{2,1,0:T(8,128)} copy(f32[8,32,128]{2,1,0:T(8,128)} %get-tuple-element.12) | data formatting | bytes 262144
  65.6 0.0 copy-start
  65.6 1.9 %copy.24 = f32[1,8,128,128]{3,2,1,0:T(8,128)} copy(f32[1,8,128,128]{3,2,1,0:T(8,128)} %bitcast.18) | data formatting | bytes 1048576
  67.5 0.0 copy-done
  67.5 0.8 %copy.25 = f32[1,8,128,128]{3,2,1,0:T(8,128)} copy(f32[1,8,128,128]{3,2,1,0:T(8,128)S(1)} %bitcast.17) | data formatting | bytes 1048576
Async XLA Ops:
  65.6 1.9 %copy-start = (f32[8,128,128]{2,1,0:T(8,128)S(1)}, f32[8,128,128]{2,1,0:T(8,128)}, u32[]{:S(2)}) copy-start(f32[8,128,128]{2,1,0:T(8,128)} %get-tuple-element.8) | copy-start | bytes 1572868

commit v4 on v3

--- a/solution.py
+++ b/solution.py
@@ -10,7 +10,7 @@
 STEPS = 4
 HALO = 4
 PAD = 8
-VMEM_BYTES = 56 * 1024 * 1024
+VMEM_BYTES = 48 * 1024 * 1024
 
 stencil_coef = (-205.0 / 72.0, 8.0 / 5.0, -1.0 / 5.0, 8.0 / 315.0, -1.0 / 560.0)
 grad_scale = 0.0625
@@ -65,9 +65,7 @@
     grad_send,
     grad_recv,
     lam_out,
-    lap_w,
     grad_part,
-    grad_part_w,
     a2a_send,
     a2a_recv,
     swap_send,
@@ -87,6 +85,7 @@
     a, c = shot // 2, shot % 2
     b, y = dom // 2, dom % 2
     same = c == y
+    my_shot = 2 * a + y
     my_dom = 2 * b + c
     partner = (2 * a + y, 2 * b + c)
 
@@ -154,8 +153,6 @@
         (next_in, lam_next),
         (lam.at[STEPS - 1], late_out),
         (lam_out, early_out),
-        (lap.at[0], lap_w),
-        (grad_part, grad_part_w),
     ]
 
     def start_swap(i):
@@ -178,8 +175,13 @@
         start_to(here, send_buf.at[o], recv_buf.at[dom], a2a_send.at[o], a2a_recv.at[dom], to)
         return carry
 
-    lax.fori_loop(1, n_dom + 1, send_piece, 0)
     start_swap(2)
+    start_swap(3)
+
+    @pl.when(same)
+    def _():
+        lax.fori_loop(1, n_dom + 1, send_piece, 0)
+
 
     row_i = lax.broadcasted_iota(jnp.int32, (lanes, lanes), 0)
     col_i = lax.broadcasted_iota(jnp.int32, (lanes, lanes), 1)
@@ -229,6 +231,7 @@
             parts[i, k * lanes : (k + 1) * lanes, :] = part
     to_scalar.wait()
 
+    start_swap(4)
     group = depth // 2
 
     def inject_half(h, carry):
@@ -246,7 +249,6 @@
 
     lax.fori_loop(0, 2, inject_half, 0)
 
-    start_swap(3)
     src_plane = ints_s[1, 0] - my_dom * depth
     cell = lax.broadcasted_iota(jnp.int32, (width, lanes), 0) * lanes + lax.broadcasted_iota(
         jnp.int32, (width, lanes), 1
@@ -330,9 +332,6 @@
         if n is not None:
             send_up(ch, n)
 
-    for h in range(n_dom):
-        wait_got(recv_buf.at[h], a2a_recv.at[h])
-    start_swap(4)
     rows = recv_buf.shape[1]
     half = n_dom // 2
     per = max(1, rows // width)
@@ -354,32 +353,32 @@
             e_buf[0, z, pl.ds(at + PAD, cut), :] = newer
         return carry
 
-    lax.fori_loop(0, half, unpack, 0)
-    send_down(0, 0)
-    send_up(0, 0)
-    lateral(0, lap.at[0])
+    def first_forward():
+        for h in range(n_dom):
+            wait_got(recv_buf.at[h], a2a_recv.at[h])
+        lax.fori_loop(0, half, unpack, 0)
+        send_down(0, 0)
+        send_up(0, 0)
+        lateral(0, lap.at[0])
 
     def forward_step(n):
-        last = n == STEPS - 1
         wait_halo(0, n)
 
         def plane(z, carry):
             value = lap[n, z] + vertical(0, n, z)
             lap[n, z] = value
-            if not last:
-                older = u_first[z] if n == 0 else v_buf[0, n - 1, z + HALO]
-                amount = floats_w[n : n + 1, n_rec : n_rec + lanes] * jnp.where(src_plane == z, 1.0, 0.0)
-                put_field(
-                    0,
-                    n + 1,
-                    z,
-                    2.0 * v_buf[0, n, z + HALO] - older + speed[z] * value + src_mask[...] * amount,
-                )
+            older = u_first[z] if n == 0 else v_buf[0, n - 1, z + HALO]
+            amount = floats_w[n : n + 1, n_rec : n_rec + lanes] * jnp.where(src_plane == z, 1.0, 0.0)
+            put_field(
+                0,
+                n + 1,
+                z,
+                2.0 * v_buf[0, n, z + HALO] - older + speed[z] * value + src_mask[...] * amount,
+            )
             return carry
 
-        sweep(plane, 0, None if last else n + 1)
-        if not last:
-            lateral(0, lap.at[n + 1])
+        sweep(plane, 0, n + 1)
+        lateral(0, lap.at[n + 1])
 
     def adjoint_step(n):
         last = n == STEPS - 1
@@ -398,7 +397,6 @@
         sweep(plane, 1, None if last else n + 1)
 
     wait_swap(2)
-    forward_step(0)
     wait_swap(3)
 
     def first_scaled(z, carry):
@@ -406,56 +404,67 @@
         return carry
 
     sweep(first_scaled, 1, 0)
+
+    @pl.when(jnp.logical_not(same))
+    def _():
+        lax.fori_loop(1, n_dom + 1, send_piece, 0)
+
     lateral(1, lap_adj)
-    forward_step(1)
     wait_swap(4)
-    start_swap(7)
     adjoint_step(0)
     lateral(1, lap_adj)
-    forward_step(2)
+    first_forward()
     adjoint_step(1)
     lateral(1, lap_adj)
-    forward_step(3)
-
-    def early_terms(z, carry):
-        total = lam[0, z] * lap[STEPS - 1, z]
-        for k in range(1, STEPS - 1):
-            total = total + lam[k, z] * lap[STEPS - 1 - k, z]
-        grad_part[z] = total
-        return carry
-
-    lax.fori_loop(0, depth, early_terms, 0)
-    start_swap(8)
+    forward_step(0)
     adjoint_step(2)
     start_swap(5)
     lateral(1, lap_adj)
+    forward_step(1)
     adjoint_step(3)
     start_swap(6)
-
-    wait_swap(7)
-    wait_swap(8)
-    wait_swap(5)
+    forward_step(2)
+
+    def early_terms(z, carry):
+        total = lam[1, z] * lap[STEPS - 2, z]
+        for k in range(2, STEPS):
+            total = total + lam[k, z] * lap[STEPS - 1 - k, z]
+        grad_part[z] = total
+        return carry
+
+    lax.fori_loop(0, depth, early_terms, 0)
+    wait_halo(0, STEPS - 1)
 
     def gradient(z, carry):
-        total = grad_scale * (grad_part_w[z] + late_out[z] * lap_w[z])
+        value = lap[STEPS - 1, z] + vertical(0, STEPS - 1, z)
+        total = grad_scale * (grad_part[z] + lam[0, z] * value)
         for j in range(n_shot):
             grad_send[j, z] = total[j * share : (j + 1) * share]
         return carry
 
-    lax.fori_loop(0, depth, gradient, 0)
-
-    def share_to(i):
-        j = (shot + i) % n_shot
-        return remote(grad_send.at[j], grad_recv.at[shot], grad_ssem.at[j], grad_rsem.at[shot], (j, dom))
-
-    for i in range(1, n_shot):
-        share_to(i).start()
-    total = grad_send[shot]
-    for i in range(1, n_shot):
-        j = (shot + i) % n_shot
-        wait_got(grad_recv.at[j], grad_rsem.at[j])
-        total = total + grad_recv[j]
-    grad_out[...] = total
+    def share_to(j, h):
+        planes = pl.ds(h * group, group)
+        return (
+            jnp.logical_and(same, shot == j),
+            grad_send.at[j, planes],
+            grad_recv.at[my_shot, planes],
+            grad_ssem.at[2 * j + h],
+            grad_rsem.at[2 * my_shot + h],
+            (j, my_dom),
+        )
+
+    for h in range(2):
+        lax.fori_loop(h * group, (h + 1) * group, gradient, 0)
+        for j in range(n_shot):
+            start_to(*share_to(j, h))
+    for h in range(2):
+        for j in range(n_shot):
+            wait_got(grad_recv.at[j, pl.ds(h * group, group)], grad_rsem.at[2 * j + h])
+        total = grad_recv[0, h * group : (h + 1) * group]
+        for j in range(1, n_shot):
+            total = total + grad_recv[j, h * group : (h + 1) * group]
+        grad_out[h * group : (h + 1) * group] = total
+    wait_swap(5)
     wait_swap(6)
 
     for i, (src, dst) in enumerate(swaps):
@@ -467,8 +476,9 @@
         return carry
 
     lax.fori_loop(0, n_dom, piece_sent, 0)
-    for i in range(1, n_shot):
-        share_to(i).wait_send()
+    for h in range(2):
+        for j in range(n_shot):
+            wait_sent(*share_to(j, h))
 
     @pl.when(has_down)
     def _():
@@ -506,7 +516,7 @@
     pieces = parked[0].reshape(n_dom, rows, lanes)
     vmem = pl.BlockSpec(memory_space=pltpu.VMEM)
     smem = pl.BlockSpec(memory_space=pltpu.SMEM)
-    anywhere = pl.BlockSpec(memory_space=pl.ANY)
+    hbm = pl.BlockSpec(memory_space=pltpu.HBM)
     slab = (depth, width, lanes)
     dma = pltpu.SemaphoreType.DMA
     share = width // n_shot
@@ -517,7 +527,7 @@
             jax.ShapeDtypeStruct(slab, F32),
             jax.ShapeDtypeStruct(slab, F32),
         ],
-        in_specs=[vmem] + [smem] * 5 + [vmem] + [anywhere] * 3 + [vmem] * 2,
+        in_specs=[vmem] + [smem] * 5 + [vmem] + [hbm] * 3 + [vmem] * 2,
         out_specs=[vmem] * 3,
         scratch_shapes=[
             pltpu.VMEM((n_dom, rows, lanes), BF16),
@@ -543,16 +553,14 @@
             pltpu.VMEM((n_shot, depth, share, lanes), F32),
             pltpu.VMEM(slab, F32),
             pltpu.VMEM(slab, F32),
-            pltpu.VMEM(slab, F32),
-            pltpu.VMEM(slab, F32),
             dma((n_dom,)),
             dma((n_dom,)),
-            dma((9,)),
-            dma((9,)),
+            dma((7,)),
+            dma((7,)),
             dma((4 * STEPS,)),
             dma((4 * STEPS,)),
-            dma((n_shot,)),
-            dma((n_shot,)),
+            dma((2 * n_shot,)),
+            dma((2 * n_shot,)),
             dma,
         ],
         compiler_params=pltpu.CompilerParams(

time: 68.7 us -> 69.9 us (1.017)
  Pallas kernels: 60.2 us -> 61.7 us
    pallas_call x1, Pallas kernels: 60.2 us -> 61.7 us  [per_device(): pl.pallas_call(functools.partial(window_kernel, n_shot, n_dom), out_shape...]
    unnamed x6 -> x22, local copies, waits for them, and re-layouts: 6.2 us -> 5.88 us
where the time goes in v4:
time: 69.9 us; the launch traced here: 69.6 us
  Pallas kernels  61.7 us (88%)
  local copies, waits for them, and re-layouts  5.88 us (8%)
  between operations  2.02 us (3%)
    pallas_call x1, Pallas kernels, per_device(): pl.pallas_call(functools.partial(window_kernel, n_shot, n_dom), out_shape...  61.7 us
    unnamed x22, local copies, waits for them, and re-layouts  5.88 us

profile of v4, /device:TPU:11, one launch (start us, length us, event | category | flops | bytes accessed | tf_op | source)
XLA Modules:
  0.0 69.6 jit_solution(565639951633712479)
XLA Ops:
  1.9 0.0 copy-start.4
  1.9 0.0 copy-start.5
  1.9 0.0 copy-start
  2.0 0.0 copy-start.1
  2.0 1.2 %copy.17 = bf16[1,8,256,128]{3,2,1,0:T(8,128)(2,1)S(1)} copy(bf16[1,8,256,128]{3,1,2,0:T(8,128)(2,1)} %bitcast.26) | data formatting | bytes 1048576
  3.2 0.0 copy-start.6
  3.2 0.0 copy-start.7
  3.2 0.0 copy-start.8
  3.2 0.0 copy-done.4
  3.2 0.0 copy-done.5
  3.2 0.0 copy-done
  3.2 0.1 copy-done.1
  3.3 0.5 copy-done.6
  3.9 0.0 copy-done.7
  3.9 0.0 copy-done.8
  3.9 0.0 copy-start.2
  3.9 1.0 %copy-done.2 = f32[1,8,128,128]{3,2,1,0:T(8,128)S(1)} copy-done((f32[1,8,128,128]{3,2,1,0:T(8,128)S(1)}, f32[1,8,128,128]{3,2,1,0:T(8,128)}, u32[]{:S(2)}) %copy-start.2) | copy-done | bytes 524312
  4.9 0.0 copy-start.3
  4.9 0.7 %copy-done.3 = f32[1,4,1024]{2,1,0:T(4,128)S(1)} copy-done((f32[1,4,1024]{2,1,0:T(4,128)S(1)}, f32[1,4,1024]{2,1,0:T(4,128)}, u32[]{:S(2)}) %copy-start.3) | copy-done | bytes 16408
  5.6 61.7 %adjoint_window.1 = (f32[8,32,128]{2,1,0:T(8,128)S(1)}, f32[8,128,128]{2,1,0:T(8,128)S(1)}, f32[8,128,128]{2,1,0:T(8,128)S(1)}) custom-call(bf16[8,256,128]{2,1,0:T(8,128)(2,1)S(1)} %bitcast.15, s32[8]{0:T(128)S(1)} %bitcast.23, s32[8]{0:T(128)S(1)} %bitcast.24, f32[3]{0:T(128)S(1)} %bitcast.25, s32[1]{0:T(128)S(6)} %copy.21.src_depth, s32[1]{0:T(128)S(6)} %copy.22.src_row, ...), custom_call_target="tpu_custom_call" | custom-call | tf_op jit(solution)/shard_map/adjoint_window/pallas_call | solution.py:523
  67.3 0.7 copy.23
  68.0 0.8 %copy.24 = f32[1,8,128,128]{3,2,1,0:T(8,128)} copy(f32[1,8,128,128]{3,2,1,0:T(8,128)S(1)} %bitcast.17) | data formatting | bytes 1048576
  68.8 0.8 %copy.25 = f32[1,8,128,128]{3,2,1,0:T(8,128)} copy(f32[1,8,128,128]{3,2,1,0:T(8,128)S(1)} %bitcast.16) | data formatting | bytes 1048576
Async XLA Ops:
  1.9 1.3 %copy-start.4 = (s32[1024]{0:T(1024)S(1)}, s32[1024]{0:T(1024)}, u32[]{:S(2)}) copy-start(s32[1024]{0:T(1024)} %param.21) | copy-start | bytes 12292
  1.9 1.3 %copy-start.5 = (s32[1024]{0:T(1024)S(1)}, s32[1024]{0:T(1024)}, u32[]{:S(2)}) copy-start(s32[1024]{0:T(1024)} %param.22) | copy-start | bytes 12292
  1.9 1.3 %copy-start = (f32[8,128,128]{2,1,0:T(8,128)S(1)}, f32[8,128,128]{2,1,0:T(8,128)}, u32[]{:S(2)}) copy-start(f32[8,128,128]{2,1,0:T(8,128)} %speed_in.1) | copy-start | bytes 1572868
  2.0 1.4 %copy-start.1 = (f32[1,8,128,128]{3,2,1,0:T(8,128)S(1)}, f32[1,8,128,128]{3,2,1,0:T(8,128)}, u32[]{:S(2)}) copy-start(f32[1,8,128,128]{3,2,1,0:T(8,128)} %param.16) | copy-start | bytes 1572868
  3.2 0.7 copy-start.6
  3.2 0.7 copy-start.7
  3.2 0.7 copy-start.8
  3.9 1.0 %copy-start.2 = (f32[1,8,128,128]{3,2,1,0:T(8,128)S(1)}, f32[1,8,128,128]{3,2,1,0:T(8,128)}, u32[]{:S(2)}) copy-start(f32[1,8,128,128]{3,2,1,0:T(8,128)} %param.17) | copy-start | bytes 1572868
  4.9 0.7 %copy-start.3 = (f32[1,4,1024]{2,1,0:T(4,128)S(1)}, f32[1,4,1024]{2,1,0:T(4,128)}, u32[]{:S(2)}) copy-start(f32[1,4,1024]{2,1,0:T(4,128)} %param.23) | copy-start | bytes 49156

commit v5 on v4

--- a/solution.py
+++ b/solution.py
@@ -75,6 +75,8 @@
     grad_ssem,
     grad_rsem,
     local_sem,
+    pass_send,
+    pass_recv,
 ):
     depth, width, lanes = speed_in.shape
     groups = n_shot // 2
@@ -175,7 +177,21 @@
         start_to(here, send_buf.at[o], recv_buf.at[dom], a2a_send.at[o], a2a_recv.at[dom], to)
         return carry
 
-    start_swap(2)
+    part = depth // 2
+    mine = pl.ds((a % 2) * part, part)
+    theirs = pl.ds((1 - a % 2) * part, part)
+    next_group = (2 * (a + 1 - 2 * (a % 2)) + c, dom)
+    half_speed = remote(speed_in.at[mine], speed.at[mine], swap_send.at[2], swap_recv.at[2], partner)
+    pass_speed = remote(speed.at[mine], speed.at[mine], pass_send.at[0], pass_recv.at[0], next_group)
+
+    @pl.when(same)
+    def _():
+        pltpu.make_async_copy(speed_in, speed, swap_recv.at[2]).start()
+
+    @pl.when(jnp.logical_not(same))
+    def _():
+        half_speed.start()
+
     start_swap(3)
 
     @pl.when(same)
@@ -224,6 +240,12 @@
     wait_swap(1)
     to_scalar = pltpu.make_async_copy(ints_w, ints_s, local_sem)
     to_scalar.start()
+
+    @pl.when(jnp.logical_not(same))
+    def _():
+        wait_got(speed.at[mine], swap_recv.at[2])
+        pass_speed.start()
+
     lane_hit = lax.broadcasted_iota(jnp.int32, (lanes, n_rec), 0) == rec_lane
     for k in range(STEPS):
         amounts = jnp.where(lane_hit, floats_w[k : k + 1, 0:n_rec], 0.0)
@@ -396,7 +418,14 @@
 
         sweep(plane, 1, None if last else n + 1)
 
-    wait_swap(2)
+    @pl.when(same)
+    def _():
+        wait_got(speed, swap_recv.at[2])
+
+    @pl.when(jnp.logical_not(same))
+    def _():
+        wait_got(speed.at[theirs], pass_recv.at[0])
+
     wait_swap(3)
 
     def first_scaled(z, carry):
@@ -467,7 +496,14 @@
     wait_swap(5)
     wait_swap(6)
 
+    @pl.when(jnp.logical_not(same))
+    def _():
+        half_speed.wait_send()
+        pass_speed.wait_send()
+
     for i, (src, dst) in enumerate(swaps):
+        if i == 2:
+            continue
         wait_sent(same, src, dst, swap_send.at[i], swap_recv.at[i], partner)
 
     def piece_sent(o, carry):
@@ -562,6 +598,8 @@
             dma((2 * n_shot,)),
             dma((2 * n_shot,)),
             dma,
+            dma((1,)),
+            dma((1,)),
         ],
         compiler_params=pltpu.CompilerParams(
             collective_id=0, has_side_effects=True, vmem_limit_bytes=VMEM_BYTES

time: 69.9 us -> 67.1 us (0.960)
  Pallas kernels: 61.7 us -> 58.9 us
    pallas_call x1, Pallas kernels: 61.7 us -> 58.9 us  [per_device(): pl.pallas_call(functools.partial(window_kernel, n_shot, n_dom), out_shape...]
where the time goes in v5:
time: 67.1 us; the launch traced here: 66.8 us
  Pallas kernels  58.9 us (88%)
  local copies, waits for them, and re-layouts  5.88 us (9%)
  between operations  2.02 us (3%)
    pallas_call x1, Pallas kernels, per_device(): pl.pallas_call(functools.partial(window_kernel, n_shot, n_dom), out_shape...  58.9 us
    unnamed x22, local copies, waits for them, and re-layouts  5.88 us

profile of v5, /device:TPU:11, one launch (start us, length us, event | category | flops | bytes accessed | tf_op | source)
XLA Modules:
  0.0 66.8 jit_solution(4104967009134138600)
XLA Ops:
  1.9 0.0 copy-start.4
  1.9 0.0 copy-start.5
  1.9 0.0 copy-start
  2.0 0.0 copy-start.1
  2.0 1.2 %copy.17 = bf16[1,8,256,128]{3,2,1,0:T(8,128)(2,1)S(1)} copy(bf16[1,8,256,128]{3,1,2,0:T(8,128)(2,1)} %bitcast.26) | data formatting | bytes 1048576
  3.2 0.0 copy-start.6
  3.2 0.0 copy-start.7
  3.2 0.0 copy-start.8
  3.2 0.0 copy-done.4
  3.2 0.0 copy-done.5
  3.2 0.0 copy-done
  3.2 0.1 copy-done.1
  3.3 0.5 copy-done.6
  3.9 0.0 copy-done.7
  3.9 0.0 copy-done.8
  3.9 0.0 copy-start.2
  3.9 1.0 %copy-done.2 = f32[1,8,128,128]{3,2,1,0:T(8,128)S(1)} copy-done((f32[1,8,128,128]{3,2,1,0:T(8,128)S(1)}, f32[1,8,128,128]{3,2,1,0:T(8,128)}, u32[]{:S(2)}) %copy-start.2) | copy-done | bytes 524312
  4.9 0.0 copy-start.3
  4.9 0.7 %copy-done.3 = f32[1,4,1024]{2,1,0:T(4,128)S(1)} copy-done((f32[1,4,1024]{2,1,0:T(4,128)S(1)}, f32[1,4,1024]{2,1,0:T(4,128)}, u32[]{:S(2)}) %copy-start.3) | copy-done | bytes 16408
  5.6 58.9 %adjoint_window.1 = (f32[8,32,128]{2,1,0:T(8,128)S(1)}, f32[8,128,128]{2,1,0:T(8,128)S(1)}, f32[8,128,128]{2,1,0:T(8,128)S(1)}) custom-call(bf16[8,256,128]{2,1,0:T(8,128)(2,1)S(1)} %bitcast.15, s32[8]{0:T(128)S(1)} %bitcast.23, s32[8]{0:T(128)S(1)} %bitcast.24, f32[3]{0:T(128)S(1)} %bitcast.25, s32[1]{0:T(128)S(6)} %copy.21.src_depth, s32[1]{0:T(128)S(6)} %copy.22.src_row, ...), custom_call_target="tpu_custom_call" | custom-call | tf_op jit(solution)/shard_map/adjoint_window/pallas_call | solution.py:559
  64.6 0.7 copy.23
  65.2 0.8 %copy.24 = f32[1,8,128,128]{3,2,1,0:T(8,128)} copy(f32[1,8,128,128]{3,2,1,0:T(8,128)S(1)} %bitcast.17) | data formatting | bytes 1048576
  66.0 0.8 %copy.25 = f32[1,8,128,128]{3,2,1,0:T(8,128)} copy(f32[1,8,128,128]{3,2,1,0:T(8,128)S(1)} %bitcast.16) | data formatting | bytes 1048576
Async XLA Ops:
  1.9 1.3 %copy-start.4 = (s32[1024]{0:T(1024)S(1)}, s32[1024]{0:T(1024)}, u32[]{:S(2)}) copy-start(s32[1024]{0:T(1024)} %param.21) | copy-start | bytes 12292
  1.9 1.3 %copy-start.5 = (s32[1024]{0:T(1024)S(1)}, s32[1024]{0:T(1024)}, u32[]{:S(2)}) copy-start(s32[1024]{0:T(1024)} %param.22) | copy-start | bytes 12292
  1.9 1.3 %copy-start = (f32[8,128,128]{2,1,0:T(8,128)S(1)}, f32[8,128,128]{2,1,0:T(8,128)}, u32[]{:S(2)}) copy-start(f32[8,128,128]{2,1,0:T(8,128)} %speed_in.1) | copy-start | bytes 1572868
  2.0 1.4 %copy-start.1 = (f32[1,8,128,128]{3,2,1,0:T(8,128)S(1)}, f32[1,8,128,128]{3,2,1,0:T(8,128)}, u32[]{:S(2)}) copy-start(f32[1,8,128,128]{3,2,1,0:T(8,128)} %param.16) | copy-start | bytes 1572868
  3.2 0.7 %copy-start.6 = (s32[1,1,8]{2,1,0:T(1,128)S(1)}, s32[1,1,8]{2,1,0:T(1,128)}, u32[]{:S(2)}) copy-start(s32[1,1,8]{2,1,0:T(1,128)} %param.13) | copy-start | bytes 100
  3.2 0.7 %copy-start.7 = (s32[1,1,8]{2,1,0:T(1,128)S(1)}, s32[1,1,8]{2,1,0:T(1,128)}, u32[]{:S(2)}) copy-start(s32[1,1,8]{2,1,0:T(1,128)} %param.14) | copy-start | bytes 100
  3.2 0.7 %copy-start.8 = (f32[1,3]{1,0:T(1,128)S(1)}, f32[1,3]{1,0:T(1,128)}, u32[]{:S(2)}) copy-start(f32[1,3]{1,0:T(1,128)} %param.18) | copy-start | bytes 40
  3.9 1.0 %copy-start.2 = (f32[1,8,128,128]{3,2,1,0:T(8,128)S(1)}, f32[1,8,128,128]{3,2,1,0:T(8,128)}, u32[]{:S(2)}) copy-start(f32[1,8,128,128]{3,2,1,0:T(8,128)} %param.17) | copy-start | bytes 1572868
  4.9 0.7 %copy-start.3 = (f32[1,4,1024]{2,1,0:T(4,128)S(1)}, f32[1,4,1024]{2,1,0:T(4,128)}, u32[]{:S(2)}) copy-start(f32[1,4,1024]{2,1,0:T(4,128)} %param.23) | copy-start | bytes 49156
